TPU v7x, 32 devices: a whole 2x2x4 slice. The times are simulated.
32 devices in a mesh: batch: 16 (over z, y, core), heads: 2 (over x).
Axes of the slice: x: 2, y: 2, z: 4, core: 2. Of those that a mesh axis runs over, the one named last changes fastest.
Arguments:
- tokens: bfloat16 [86016, 128], P(('batch', 'heads')), may hold values from -6 to 6
- image_bands: int32 [16, 24], P('batch'), may hold values from 0 to 14, as said below
- cotangent: bfloat16 [86016, 128], P(('batch', 'heads')), may hold values from -6 to 6
- front_gains: float32 [2, 128], replicated, may hold values from 0.1 to 1.9
- front_shifts: float32 [4, 128], replicated, may hold values from -2 to 2
- query_w: bfloat16 [128, 128], P(None, 'heads'), may hold values from -1 to 1
- coarse_conv: bfloat16 [2048, 128], replicated, may hold values from -0.125 to 0.125
- coarse_gain: float32 [128], replicated, may hold values from 0.1 to 1.9
- coarse_shifts: float32 [3, 128], replicated, may hold values from -2 to 2
- coarse_kv: bfloat16 [128, 128], replicated, may hold values from -0.5 to 0.5
- coarse_taps: float32 [9, 64], replicated, may hold values from -2 to 2
- fine_conv: bfloat16 [512, 128], replicated, may hold values from -0.25 to 0.25
- fine_gain: float32 [128], replicated, may hold values from 0.1 to 1.9
- fine_shifts: float32 [3, 128], replicated, may hold values from -2 to 2
- fine_kv: bfloat16 [128, 128], replicated, may hold values from -0.5 to 0.5
- fine_taps: float32 [9, 64], replicated, may hold values from -2 to 2
- proj_w: bfloat16 [128, 128], replicated, may hold values from -1.5 to 1.5
- hidden_shifts: float32 [2, 1024], P(None, 'heads'), may hold values from -2 to 2
- fc1_w: bfloat16 [128, 1024], P(None, 'heads'), may hold values from -0.5 to 0.5
- depth_taps: float32 [9, 1024], P(None, 'heads'), may hold values from -2 to 2
- fc2_w: bfloat16 [1024, 128], P('heads'), may hold values from -0.1875 to 0.1875
Outputs:
- output: bfloat16 [86016, 128], P(('batch', 'heads'))
- tokens_grad: float32 [86016, 128], P(('batch', 'heads'))
- front_gains_grad: float32 [2, 128], replicated
- front_shifts_grad: float32 [4, 128], replicated
- query_w_grad: float32 [128, 128], P(None, 'heads')
- coarse_conv_grad: float32 [2048, 128], replicated
- coarse_gain_grad: float32 [128], replicated
- coarse_shifts_grad: float32 [3, 128], replicated
- coarse_kv_grad: float32 [128, 128], replicated
- coarse_taps_grad: float32 [9, 64], replicated
- fine_conv_grad: float32 [512, 128], replicated
- fine_gain_grad: float32 [128], replicated
- fine_shifts_grad: float32 [3, 128], replicated
- fine_kv_grad: float32 [128, 128], replicated
- fine_taps_grad: float32 [9, 64], replicated
- proj_w_grad: float32 [128, 128], replicated
- hidden_shifts_grad: float32 [2, 1024], P(None, 'heads')
- fc1_w_grad: float32 [128, 1024], P(None, 'heads')
- depth_taps_grad: float32 [9, 1024], P(None, 'heads')
- fc2_w_grad: float32 [1024, 128], P('heads')
Inputs may be any that keep to these rules, and one draw needn't show every extreme that they name: `image_bands`: each row lists the heights, in bands of 4 rows of 56 patches, of one group's images, nonzero heights first and zeros after; a row adds up to at most 24; one row adds up to exactly 24 and begins with an image of 14 bands.
All inputs are finite; a program needn't handle non-finite values.
Results may differ from a plain program's by a relative error of at most 0.018.
Values may be sent and summed in bfloat16 or wider, within the bound.
A program may use at most 192 MiB of HBM per device.

v0:
```python
import jax
import jax.numpy as jnp
from jax import lax
from jax.sharding import PartitionSpec as P

W = 56


EPS = 1e-06


def inner(left, right):
    return lax.dot_general(
        left, right, (((0,), (0,)), ((), ())), preferred_element_type=jnp.float32
    )


def outer_t(left, right):
    return lax.dot_general(
        left, right, (((1,), (1,)), ((), ())), preferred_element_type=jnp.float32
    )


def band_images(heights, band_count):
    ends = jnp.cumsum(heights)
    band_index = jnp.arange(band_count, dtype=jnp.int32)
    image_num = jnp.sum((band_index[:, None] >= ends[None, :]).astype(jnp.int32), axis=1)
    return jnp.where(band_index < ends[-1], image_num, -1)


def depthwise_ext(ext_grid, tap_weights, ext_ids):
    grid_rows, grid_cols = (ext_grid.shape[0] - 2, ext_grid.shape[1])
    padded = jnp.pad(ext_grid, ((0, 0), (1, 1), (0, 0)))
    row_ids = ext_ids[1:-1]
    result = jnp.zeros((grid_rows,) + ext_grid.shape[1:], ext_grid.dtype)
    for above in range(3):
        same_image = (ext_ids[above : above + grid_rows] == row_ids).astype(ext_grid.dtype)[
            :, None, None
        ]
        for across in range(3):
            result = (
                result
                + padded[above : above + grid_rows, across : across + grid_cols]
                * tap_weights[3 * above + across]
                * same_image
            )
    return result


def depthwise(grid, tap_weights, row_ids):
    return depthwise_ext(
        jnp.pad(grid, ((1, 1), (0, 0), (0, 0))),
        tap_weights,
        jnp.pad(row_ids, 1, constant_values=-2),
    )


def tap_grads_ext(ext_grid, grad_grid, ext_ids):
    grid_rows, grid_cols = (ext_grid.shape[0] - 2, ext_grid.shape[1])
    padded = jnp.pad(ext_grid, ((0, 0), (1, 1), (0, 0)))
    row_ids = ext_ids[1:-1]
    collected = []
    for above in range(3):
        same_image = (ext_ids[above : above + grid_rows] == row_ids).astype(ext_grid.dtype)[
            :, None, None
        ]
        for across in range(3):
            shifted = padded[above : above + grid_rows, across : across + grid_cols]
            collected.append(jnp.sum(shifted * grad_grid * same_image, axis=(0, 1)))
    return jnp.stack(collected)


def tap_grads(grid, grad_grid, row_ids):
    return tap_grads_ext(
        jnp.pad(grid, ((1, 1), (0, 0), (0, 0))), grad_grid, jnp.pad(row_ids, 1, constant_values=-2)
    )


def patchify(grid, stride_len):
    grid_rows, grid_cols, channels = grid.shape
    blocks = grid.reshape(
        grid_rows // stride_len, stride_len, grid_cols // stride_len, stride_len, channels
    )
    blocks = blocks.transpose(0, 2, 1, 3, 4)
    return blocks.reshape(
        grid_rows // stride_len * (grid_cols // stride_len), stride_len * stride_len * channels
    )


def unpatchify(patch_grad, grid_rows, grid_cols, stride_len):
    channels = patch_grad.shape[1] // (stride_len * stride_len)
    blocks = patch_grad.reshape(
        grid_rows // stride_len, grid_cols // stride_len, stride_len, stride_len, channels
    )
    return blocks.transpose(0, 2, 1, 3, 4).reshape(grid_rows * grid_cols, channels)


def norm_parts(values, norm_gain, norm_shift):
    mean_val = jnp.mean(values, axis=-1, keepdims=True)
    centred = values - mean_val
    inverse = lax.rsqrt(jnp.mean(centred * centred, axis=-1, keepdims=True) + EPS)
    scaled = centred * inverse
    return (scaled * norm_gain + norm_shift, scaled, inverse)


def norm_back(grad_out, scaled, inverse, norm_gain):
    grad_scaled = grad_out * norm_gain
    centre_term = jnp.mean(grad_scaled, axis=-1, keepdims=True)
    scale_term = jnp.mean(grad_scaled * scaled, axis=-1, keepdims=True)
    return inverse * (grad_scaled - centre_term - scaled * scale_term)


def gelu_value(values):
    return jax.nn.gelu(values, approximate=False)


def gelu_slope(values):
    return (
        0.5 * (1.0 + lax.erf(values * 0.7071067811865476))
        + values * jnp.exp(-0.5 * values * values) * 0.3989422804014327
    )


def branch_cells(normed_b, stride_len, weights, grid_cols):
    conv_w, norm_gain, shifts, kv_weight, tap_weights = weights
    grid_rows = normed_b.shape[0] // grid_cols
    half_width = kv_weight.shape[1] // 2
    patches = patchify(normed_b.reshape(grid_rows, grid_cols, -1), stride_len)
    reduced = jnp.dot(patches, conv_w, preferred_element_type=jnp.float32) + shifts[0]
    normed_red, scaled, inverse = norm_parts(reduced, norm_gain, shifts[1])
    active = gelu_value(normed_red).astype(jnp.bfloat16)
    key_value = jnp.dot(active, kv_weight, preferred_element_type=jnp.float32)
    key_part = key_value[:, :half_width].astype(jnp.bfloat16)
    value_pre = key_value[:, half_width:] + shifts[2, :half_width]
    return (key_part, value_pre, (patches, normed_red, scaled, inverse, active))


def branch_values(value_pre, key_rows, stride_len, grid_cols, weights):
    shifts, tap_weights = (weights[2], weights[4])
    half_width = value_pre.shape[1]
    value_grid = value_pre.reshape(key_rows.shape[0], grid_cols // stride_len, half_width)
    local_term = depthwise(value_grid, tap_weights, key_rows).reshape(-1, half_width)
    value_part = (value_pre + local_term + shifts[2, half_width:]).astype(jnp.bfloat16)
    return (value_grid, value_part)


def attend_forward(queries, key_part, value_part, query_ids, key_ids, block_rows):
    head_width = key_part.shape[1] // 2
    block_count = queries.shape[0] // block_rows
    key_head_rows = key_part.reshape(-1, 2, head_width)
    value_head_rows = value_part.reshape(-1, 2, head_width)

    def one_block(entry_now):
        query_block_rows, block_ids = entry_now
        score_matrix = jnp.einsum(
            "lfq,tfq->flt", query_block_rows, key_head_rows, preferred_element_type=jnp.float32
        ) * head_width ** (-0.5)
        allowed = (block_ids[:, None] == key_ids[None, :]) & (block_ids[:, None] >= 0)
        score_matrix = jnp.where(allowed[None], score_matrix, -1000000000.0)
        largest = jnp.max(score_matrix, axis=-1, keepdims=True)
        expo = jnp.exp(score_matrix - largest)
        totals = jnp.sum(expo, axis=-1, keepdims=True)
        softmax_weight_rows = (expo / totals).astype(jnp.bfloat16)
        mixed_out = jnp.einsum(
            "vyq,qvz->yvz", softmax_weight_rows, value_head_rows, preferred_element_type=jnp.float32
        )
        return (mixed_out.reshape(-1, 2 * head_width), (largest + jnp.log(totals))[:, :, 0].T)

    out_blocks, lse_blocks = lax.map(
        one_block,
        (
            queries.reshape(block_count, block_rows, 2, head_width),
            query_ids.reshape(block_count, block_rows),
        ),
    )
    return (out_blocks.reshape(-1, 2 * head_width), lse_blocks.reshape(-1, 2))


def attend_backward(
    queries, key_part, value_part, query_ids, key_ids, log_sums, out_grad, block_rows
):
    head_width = key_part.shape[1] // 2
    block_count = queries.shape[0] // block_rows
    key_head_rows = key_part.reshape(-1, 2, head_width)
    value_head_rows = value_part.reshape(-1, 2, head_width)
    scale_val = head_width ** (-0.5)

    def one_block(carry, entry_now):
        key_grad, value_grad = carry
        query_block_rows, block_ids, block_lse, gradient_block_rows = entry_now
        score_matrix = (
            jnp.einsum(
                "lfq,tfq->flt", query_block_rows, key_head_rows, preferred_element_type=jnp.float32
            )
            * scale_val
        )
        allowed = (block_ids[:, None] == key_ids[None, :]) & (block_ids[:, None] >= 0)
        score_matrix = jnp.where(allowed[None], score_matrix, -1000000000.0)
        softmax_weight_rows = jnp.exp(score_matrix - block_lse.T[:, :, None])
        prob_grad = jnp.einsum(
            "lfq,tfq->flt", gradient_block_rows, value_head_rows, preferred_element_type=jnp.float32
        )
        row_terms = jnp.sum(prob_grad * softmax_weight_rows, axis=-1, keepdims=True)
        score_gradient = (softmax_weight_rows * (prob_grad - row_terms)).astype(jnp.bfloat16)
        query_grad = (
            jnp.einsum(
                "vyq,qvz->yvz", score_gradient, key_head_rows, preferred_element_type=jnp.float32
            )
            * scale_val
        )
        key_grad = (
            key_grad
            + jnp.einsum(
                "tiw,itg->wtg", score_gradient, query_block_rows, preferred_element_type=jnp.float32
            )
            * scale_val
        )
        value_grad = value_grad + jnp.einsum(
            "tiw,itg->wtg",
            softmax_weight_rows.astype(jnp.bfloat16),
            gradient_block_rows,
            preferred_element_type=jnp.float32,
        )
        return ((key_grad, value_grad), query_grad.reshape(-1, 2 * head_width))

    initial = (
        jnp.zeros(key_head_rows.shape, jnp.float32),
        jnp.zeros(value_head_rows.shape, jnp.float32),
    )
    (key_grad, value_grad), query_blocks = lax.scan(
        one_block,
        initial,
        (
            queries.reshape(block_count, block_rows, 2, head_width),
            query_ids.reshape(block_count, block_rows),
            log_sums.reshape(block_count, block_rows, 2),
            out_grad.reshape(block_count, block_rows, 2, head_width),
        ),
    )
    return (
        key_grad.reshape(key_part.shape),
        value_grad.reshape(value_part.shape),
        query_blocks.reshape(queries.shape[0], -1),
    )


def value_back(value_grid, key_grad, value_grad, tap_weights, key_rows, row_mask):
    half_width = value_grid.shape[2]
    local_grad = value_grad.astype(jnp.bfloat16).astype(jnp.float32).reshape(value_grid.shape)
    masked_grad = local_grad * row_mask[:, None, None]
    local_tap_grad = tap_grads(value_grid, masked_grad, key_rows)
    local_shift_grad = jnp.sum(masked_grad, axis=(0, 1))
    value_in_grad = (
        (local_grad + depthwise(local_grad, tap_weights[::-1], key_rows))
        .reshape(-1, half_width)
        .astype(jnp.bfloat16)
    )
    pair_grad = jnp.concatenate([key_grad.astype(jnp.bfloat16), value_in_grad], axis=1)
    return (pair_grad, local_tap_grad, local_shift_grad)


def reduce_back(
    saved, pair_grad, local_tap_grad, local_shift_grad, weights, stride_len, grid_rows, grid_cols
):
    conv_w, norm_gain, shifts, kv_weight, tap_weights = weights
    patches, normed_red, scaled, inverse, active = saved
    half_width = kv_weight.shape[1] // 2
    kv_grad = inner(active, pair_grad)
    value_shift_grad = jnp.sum(pair_grad[:, half_width:].astype(jnp.float32), axis=0)
    active_grad = outer_t(pair_grad, kv_weight)
    normed_grad = active_grad * gelu_slope(normed_red)
    gain_grad = jnp.sum(normed_grad * scaled, axis=0)
    norm_shift_grad = jnp.sum(normed_grad, axis=0)
    reduced_grad = norm_back(normed_grad, scaled, inverse, norm_gain).astype(jnp.bfloat16)
    conv_grad = inner(patches, reduced_grad)
    conv_shift_grad = jnp.sum(reduced_grad.astype(jnp.float32), axis=0)
    input_grad = unpatchify(outer_t(reduced_grad, conv_w), grid_rows, grid_cols, stride_len)
    shifts_grad = jnp.stack(
        [conv_shift_grad, norm_shift_grad, jnp.concatenate([value_shift_grad, local_shift_grad])]
    )
    return (input_grad, (conv_grad, gain_grad, shifts_grad, kv_grad, local_tap_grad))


def norm_sum(partial_grad, scaled, inverse, norm_gain, head_side, half_rows):
    scaled_own = lax.dynamic_slice_in_dim(scaled, head_side * half_rows, half_rows, 0)
    inverse_own = lax.dynamic_slice_in_dim(inverse, head_side * half_rows, half_rows, 0)
    total_grad = lax.psum(partial_grad.astype(jnp.bfloat16), "heads").astype(jnp.float32)
    total_own = lax.dynamic_slice_in_dim(total_grad, head_side * half_rows, half_rows, 0)
    back_own = norm_back(total_own, scaled_own, inverse_own, norm_gain)
    return (back_own, jnp.sum(total_own * scaled_own, axis=0), jnp.sum(total_own, axis=0))


def per_device(
    tokens,
    image_bands,
    cotangent,
    front_gains,
    front_shifts,
    query_w,
    coarse_conv,
    coarse_gain,
    coarse_shifts,
    coarse_kv,
    coarse_taps,
    fine_conv,
    fine_gain,
    fine_shifts,
    fine_kv,
    fine_taps,
    proj_w,
    hidden_shifts,
    fc1_w,
    depth_taps,
    fc2_w,
):
    head_side = lax.axis_index("heads")
    half_rows = tokens.shape[0]
    tok_count = 2 * half_rows
    grid_cols = W
    grid_rows = tok_count // grid_cols
    band_ids = band_images(image_bands[0], grid_rows // 4)
    token_ids = jnp.repeat(band_ids, 4 * grid_cols)
    pixel_rows = jnp.repeat(band_ids, 4)
    live_mask = (token_ids >= 0).astype(jnp.float32)[:, None]
    live_own = lax.dynamic_slice_in_dim(live_mask, head_side * half_rows, half_rows, 0)
    coarse_weights = (coarse_conv, coarse_gain, coarse_shifts, coarse_kv, coarse_taps)
    fine_weights = (fine_conv, fine_gain, fine_shifts, fine_kv, fine_taps)
    own_tokens = tokens.astype(jnp.float32)
    grad_own_b = (cotangent.astype(jnp.float32) * live_own).astype(jnp.bfloat16)
    grad_own = grad_own_b.astype(jnp.float32)
    out_bias_grad = jnp.sum(grad_own, axis=0)
    block_rows = min(tok_count, 16 * grid_cols)
    full_tokens = lax.all_gather(tokens, "heads", axis=0, tiled=True).astype(jnp.float32)
    normed, scaled_front, inverse_front = norm_parts(full_tokens, front_gains[0], front_shifts[0])
    normed_b = normed.astype(jnp.bfloat16)
    query_own = jnp.dot(normed_b, query_w, preferred_element_type=jnp.float32).astype(jnp.bfloat16)

    def rate_keys(stride_len, weights):
        key_part, value_pre, saved = branch_cells(normed_b, stride_len, weights, grid_cols)
        key_rows = jnp.repeat(band_ids, 4 // stride_len)
        value_grid, value_part = branch_values(value_pre, key_rows, stride_len, grid_cols, weights)
        key_ids = jnp.repeat(key_rows, grid_cols // stride_len)
        return (key_part, value_part, value_grid, key_rows, key_ids, saved)

    def forward_branch(stride_len, weights):
        key_part, value_part, value_grid, key_rows, key_ids, saved = rate_keys(stride_len, weights)
        return attend_forward(query_own, key_part, value_part, token_ids, key_ids, block_rows)

    heads_own, log_sums = lax.cond(
        head_side == 0,
        lambda: forward_branch(4, coarse_weights),
        lambda: forward_branch(2, fine_weights),
    )
    heads_own_b = (heads_own * live_mask).astype(jnp.bfloat16)
    heads_rows = lax.all_to_all(heads_own_b, "heads", split_axis=0, concat_axis=1, tiled=True)
    middle_own = (
        own_tokens
        + jnp.dot(heads_rows, proj_w, preferred_element_type=jnp.float32)
        + front_shifts[1]
    )
    middle_full = lax.all_gather(
        middle_own.astype(jnp.bfloat16), "heads", axis=0, tiled=True
    ).astype(middle_own.dtype)
    normed_mid, scaled_mid, inverse_mid = norm_parts(middle_full, front_gains[1], front_shifts[2])
    normed_mid_b = normed_mid.astype(jnp.bfloat16)
    hidden = jnp.dot(normed_mid_b, fc1_w, preferred_element_type=jnp.float32) + hidden_shifts[0]
    hidden_grid = hidden.reshape(grid_rows, grid_cols, -1)
    spread = (
        hidden
        + depthwise(hidden_grid, depth_taps, pixel_rows).reshape(tok_count, -1)
        + hidden_shifts[1]
    )
    activated = gelu_value(spread).astype(jnp.bfloat16)
    partial_out = jnp.dot(activated, fc2_w, preferred_element_type=jnp.float32)
    mlp_own = lax.psum_scatter(
        partial_out.astype(jnp.bfloat16), "heads", scatter_dimension=0, tiled=True
    ).astype(jnp.float32)
    output = ((middle_own + mlp_own + front_shifts[3]) * live_own).astype(jnp.bfloat16)
    grad_full = lax.all_gather(grad_own_b, "heads", axis=0, tiled=True)
    fc2_grad = inner(activated, grad_full)
    spread_grad = outer_t(grad_full, fc2_w) * gelu_slope(spread)
    spread_grid = spread_grad.reshape(grid_rows, grid_cols, -1)
    depth_grad = tap_grads(hidden_grid, spread_grid, pixel_rows)
    depth_bias_grad = jnp.sum(spread_grad, axis=0)
    hidden_grad = (
        spread_grad + depthwise(spread_grid, depth_taps[::-1], pixel_rows).reshape(tok_count, -1)
    ).astype(jnp.bfloat16)
    fc1_bias_grad = jnp.sum(hidden_grad.astype(jnp.float32), axis=0)
    fc1_grad = inner(normed_mid_b, hidden_grad)
    hidden_shift_grad = jnp.stack([fc1_bias_grad, depth_bias_grad])
    mid_partial = outer_t(hidden_grad, fc1_w)
    mid_back, gain_mid_grad, shift_mid_grad = norm_sum(
        mid_partial, scaled_mid, inverse_mid, front_gains[1], head_side, half_rows
    )
    middle_grad = grad_own + mid_back
    proj_in = middle_grad.astype(jnp.bfloat16)
    proj_grad = inner(heads_rows, proj_in)
    proj_bias_grad = jnp.sum(proj_in.astype(jnp.float32), axis=0)
    heads_back = (outer_t(proj_in, proj_w) * live_own).astype(jnp.bfloat16)
    heads_grad_b = lax.all_to_all(heads_back, "heads", split_axis=1, concat_axis=0, tiled=True)

    def backward_branch(stride_len, weights, other_weights):
        key_part, value_part, value_grid, key_rows, key_ids, saved = rate_keys(stride_len, weights)
        key_grad, value_grad, query_grad = attend_backward(
            query_own, key_part, value_part, token_ids, key_ids, log_sums, heads_grad_b, block_rows
        )
        row_mask = jnp.ones((value_grid.shape[0],), jnp.float32)
        pair_grad, tap_part, tap_shift = value_back(
            value_grid, key_grad, value_grad, weights[4], key_rows, row_mask
        )
        input_grad, own_grads = reduce_back(
            saved, pair_grad, tap_part, tap_shift, weights, stride_len, grid_rows, grid_cols
        )
        empty_grads = tuple((jnp.zeros(weight.shape, jnp.float32) for weight in other_weights))
        return (query_grad, input_grad, own_grads, empty_grads)

    def backward_coarse():
        return backward_branch(4, coarse_weights, fine_weights)

    def backward_fine():
        query_grad, input_grad, own_grads, empty_grads = backward_branch(
            2, fine_weights, coarse_weights
        )
        return (query_grad, input_grad, empty_grads, own_grads)

    query_grad, kv_input_grad, coarse_grads, fine_grads = lax.cond(
        head_side == 0, backward_coarse, backward_fine
    )
    query_grad_b = query_grad.astype(jnp.bfloat16)
    query_w_grad = inner(normed_b, query_grad_b)
    front_partial = outer_t(query_grad_b, query_w) + kv_input_grad
    front_back, gain_front_grad, shift_front_grad = norm_sum(
        front_partial, scaled_front, inverse_front, front_gains[0], head_side, half_rows
    )
    tokens_grad = middle_grad + front_back
    front_gains_grad = jnp.stack([gain_front_grad, gain_mid_grad])
    front_shifts_grad = jnp.stack([shift_front_grad, proj_bias_grad, shift_mid_grad, out_bias_grad])
    coarse_conv_grad, coarse_gain_grad, coarse_shifts_grad, coarse_kv_grad, coarse_taps_grad = (
        coarse_grads
    )
    fine_conv_grad, fine_gain_grad, fine_shifts_grad, fine_kv_grad, fine_taps_grad = fine_grads
    (
        front_gains_grad,
        front_shifts_grad,
        proj_grad,
        coarse_conv_grad,
        coarse_gain_grad,
        coarse_shifts_grad,
        coarse_kv_grad,
        coarse_taps_grad,
        fine_conv_grad,
        fine_gain_grad,
        fine_shifts_grad,
        fine_kv_grad,
        fine_taps_grad,
    ) = lax.psum(
        (
            front_gains_grad,
            front_shifts_grad,
            proj_grad,
            coarse_conv_grad,
            coarse_gain_grad,
            coarse_shifts_grad,
            coarse_kv_grad,
            coarse_taps_grad,
            fine_conv_grad,
            fine_gain_grad,
            fine_shifts_grad,
            fine_kv_grad,
            fine_taps_grad,
        ),
        ("batch", "heads"),
    )
    query_w_grad, hidden_shift_grad, fc1_grad, depth_grad, fc2_grad = lax.psum(
        (query_w_grad, hidden_shift_grad, fc1_grad, depth_grad, fc2_grad), "batch"
    )
    return (
        output,
        tokens_grad,
        front_gains_grad,
        front_shifts_grad,
        query_w_grad,
        coarse_conv_grad,
        coarse_gain_grad,
        coarse_shifts_grad,
        coarse_kv_grad,
        coarse_taps_grad,
        fine_conv_grad,
        fine_gain_grad,
        fine_shifts_grad,
        fine_kv_grad,
        fine_taps_grad,
        proj_grad,
        hidden_shift_grad,
        fc1_grad,
        depth_grad,
        fc2_grad,
    )


def solution(mesh):
    return jax.shard_map(
        per_device,
        mesh=mesh,
        in_specs=(
            P(("batch", "heads"), None),
            P("batch", None),
            P(("batch", "heads"), None),
            P(),
            P(),
            P(None, "heads"),
            P(),
            P(),
            P(),
            P(),
            P(),
            P(),
            P(),
            P(),
            P(),
            P(),
            P(),
            P(None, "heads"),
            P(None, "heads"),
            P(None, "heads"),
            P("heads", None),
        ),
        out_specs=(
            P(("batch", "heads"), None),
            P(("batch", "heads"), None),
            P(),
            P(),
            P(None, "heads"),
            P(),
            P(),
            P(),
            P(),
            P(),
            P(),
            P(),
            P(),
            P(),
            P(),
            P(),
            P(None, "heads"),
            P(None, "heads"),
            P(None, "heads"),
            P("heads", None),
        ),
        check_vma=False,
    )
```

profile of v0, /device:TPU:0, one launch (start us, length us, event | category | flops | bytes accessed | tf_op | source)
XLA Modules:
  0.0 1052.6 jit_solution(2284780419443751666)
XLA Ops:
  13.7 23.7 %all-gather.4.cloned.1.call-done = bf16[5376,128]{1,0:T(8,128)(2,1)} async-done(((bf16[2688,128]{1,0:T(8,128)(2,1)}), bf16[5376,128]{1,0:T(8,128)(2,1)}) %all-gather.4.cloned.1.call-update) | async-done | bytes 1376272 | tf_op jit(solution)/shard_map/all_gather | solution.py:333
  37.4 1.8 convert_reduce_fusion.6
  39.2 4.3 fusion.275
  43.5 5.5 fusion.270
  49.0 2.8 convolution_convert_fusion.2
  52.5 54.8 %conditional.4 = (f32[6,896,64]{1,2,0:T(8,128)}, f32[6,896,2]{1,2,0:T(2,128)}) conditional(s32[]{:T(128)} %convert_element_type.339, (bf16[5376,64]{0,1:T(8,128)(2,1)}, s32[24,224]{1,0:T(8,128)}, bf16[5376,128]{1,0:T(8,128)(2,1)}, bf16[512,128]{1,0:T(8,128)(2,1)S(1)}, f32[3,128]{1,0:T(4,128)S(1)}, /*index=5*/f32[128]{0:T(128)}, ...), branch_computations={%region_4.11_spmd, %region_11.18_spmd} | conditional | flops 574759552 | bytes 55933872 | solution.py:349
  64.4 1.9 reshape.678
  67.3 1.8 copy.272
  74.1 33.2 %while.53 = (s32[]{:T(128)}, f32[6,896,64]{1,2,0:T(8,128)}, f32[6,896,2]{1,2,0:T(2,128)}, s32[6,896]{1,0:T(8,128)}, bf16[6,896,2,32]{1,3,2,0:T(8,128)(2,1)}, /*i...) while((s32[]{:T(128)}, f32[6,896,64]{1,2,0:T(8,128)}, ...), condition=%wide.region_17.17_spmd.clone, body=%wide.region_14.16_spmd.clone.sunk | while | flops 84896896 | bytes 9397461 | solution.py:169
  107.4 2.2 copy.258
  111.0 34.0 %all_to_all.35 = bf16[2,2688,64]{1,2,0:T(8,128)(2,1)S(1)} all-to-all(bf16[2,2688,64]{1,2,0:T(8,128)(2,1)S(1)} %copy.259), channel_id=1, replica_groups=mesh['batch'=16,'heads'=2] {'heads'}, dimensions={0} | all-to-all | bytes 1376256 | tf_op jit(solution)/shard_map/all_to_all | solution.py:355
  149.9 22.9 %all-gather.6.cloned.1.call-done = bf16[5376,128]{1,0:T(8,128)(2,1)} async-done(((bf16[2688,128]{1,0:T(8,128)(2,1)}), bf16[5376,128]{1,0:T(8,128)(2,1)}) %all-gather.6.cloned.1.call-update) | async-done | bytes 1376272 | tf_op jit(solution)/shard_map/all_gather | solution.py:361
  172.8 1.8 convert_reduce_fusion.5
  174.6 4.2 fusion.274
  178.9 4.6 convolution_add_fusion.4
  183.5 5.9 pad.84
  191.0 50.9 %fusion.259 = f32[96,56,512]{2,1,0:T(8,128)} fusion(f32[96,56,512]{2,1,0:T(8,128)} %bitcast.468, f32[98,56,512]{2,1,0:T(8,128)} %pad.84, f32[512]{0:T(512)S(1)} %bitcast.520, f32[512]{0:T(512)} %bitcast.522, f32[96]{0:T(128)} %get-tuple-element.1139, f32[512]{0:T(512)S(1)} %bitcast.508, f32[512]{0:T(512)S(1)} %bitcast.510, f32[512]{0:T(512)S(1)} %bitcast.512, ...), kind=kLoop, calls=%fused_computation.487 | loop fusion | flops 57802752 | bytes 55299072 | tf_op jit(solution)/shard_map/add | solution.py:42
  241.9 27.8 %fusion.247 = (bf16[5376,512]{1,0:T(8,128)(2,1)S(1)}, f32[5376,512]{1,0:T(8,128)}) fusion(f32[512]{0:T(512)S(1)} %bitcast.528, f32[5376,512]{1,0:T(8,128)} %copy-done.4, f32[96,56,512]{2,1,0:T(8,128)} %fusion.259), kind=kLoop, calls=%fused_computation.472 | loop fusion | flops 184418304 | bytes 38537216 | tf_op jit(solution)/shard_map/convert_element_type | solution.py:373
  269.8 2.3 copy-done.6
  272.2 2.7 convolution_convert_fusion.1
  275.2 23.8 %reduce-scatter.2.cloned.1.call-done = bf16[2688,128]{1,0:T(8,128)(2,1)} async-done(((bf16[5376,128]{1,0:T(8,128)(2,1)}), bf16[2688,128]{1,0:T(8,128)(2,1)}) %reduce-scatter.2.cloned.1.call-update) | async-done | bytes 688144 | tf_op jit(solution)/shard_map/reduce_scatter | solution.py:375
  298.9 3.2 convert_reduce_fusion.9
  302.3 25.0 %all-gather.8.cloned.1.call-done = bf16[5376,128]{1,0:T(8,128)(2,1)} async-done(((bf16[2688,128]{1,0:T(8,128)(2,1)}), bf16[5376,128]{1,0:T(8,128)(2,1)}) %all-gather.8.cloned.1.call-update) | async-done | bytes 1376272 | tf_op jit(solution)/shard_map/all_gather | solution.py:379
  327.3 7.5 fusion.252
  334.8 4.1 copy-done.5
  338.9 5.4 pad.87
  344.4 48.3 %fusion.237 = f32[96,56,512]{2,1,0:T(8,128)} fusion(f32[98,56,512]{2,1,0:T(8,128)} %pad.87, f32[96,56,512]{2,1,0:T(8,128)} %bitcast.471, f32[512]{0:T(512)S(1)} %bitcast.521, f32[512]{0:T(512)S(1)} %bitcast.523, f32[96]{0:T(128)S(1)} %copy-done.121, f32[512]{0:T(512)S(1)} %bitcast.509, f32[512]{0:T(512)S(1)} %bitcast.511, f32[512]{0:T(512)S(1)} %bitcast.513, ...), kind=kLoop, calls=%fused_computation.462 | loop fusion | flops 57802752 | bytes 55298816 | tf_op jit(solution)/shard_map/add | solution.py:42
  392.7 12.7 %multiply_reduce_fusion.34 = (f32[512]{0:T(512)}, f32[512]{0:T(512)}, f32[512]{0:T(512)}, bf16[5376,512]{1,0:T(8,128)(2,1)S(1)}) fusion(f32[5376,512]{1,0:T(8,128)} %copy-done.4, f32[5376,512]{1,0:T(8,128)} %copy-done.5, f32[96,56,512]{2,1,0:T(8,128)} %fusion.237), kind=kLoop, calls=%fused_computation.492 | loop fusion | flops 19266048 | bytes 38541312 | tf_op jit(solution)/shard_map/reduce_sum | solution.py:69
  405.4 2.5 copy-done.9
  407.9 2.6 convolution_convert_fusion
  410.6 4.1 fusion.272
  414.7 43.3 %all-reduce.30.cloned.1.call-done = bf16[5376,128]{1,0:T(8,128)(2,1)} async-done(((bf16[5376,128]{1,0:T(8,128)(2,1)}), bf16[5376,128]{1,0:T(8,128)(2,1)}) %all-reduce.30.cloned.1.call-update) | async-done | bytes 1376272 | tf_op jit(solution)/shard_map/psum | solution.py:287
  457.9 2.9 fusion.289
  460.9 3.9 convert_reduce_fusion.10
  467.4 3.5 all-to-all-start.1
  471.7 9.3 all-to-all-done.1
  481.8 84.1 %conditional.5 = (f32[5376,128]{1,0:T(8,128)S(1)}, f32[2048,128]{1,0:T(8,128)}, f32[128]{0:T(128)S(1)}, f32[3,128]{1,0:T(4,128)S(1)}, f32[128,128]{1,0:T(8,128)S...) conditional(s32[]{:T(128)} %convert_element_type.339, ...), branch_computations={%region_24.46_spmd, %region_46.68_spmd} | conditional | flops 1482084864 | bytes 212207968
  490.7 1.9 copy.247
  499.7 1.8 fusion.208
  504.3 2.6 reshape.700
  506.9 2.1 copy.250
  509.1 1.7 reshape.703
  512.2 39.6 %while.55 = (s32[]{:T(128)}, f32[336,2,32]{0,2,1:T(8,128)S(1)}, f32[336,2,32]{0,2,1:T(8,128)S(1)}, bf16[6,896,64]{1,2,0:T(8,128)(2,1)}, bf16[6,896,2,32]{1,3,2,0...) while((s32[]{:T(128)}, f32[336,2,32]{0,2,1:T(8,128)S(1)}, ...), condition=%wide.region_51.51_spmd.clone, body=%wide.region_49.50_spmd.clone.sunk | while | flops 198918272 | bytes 20017420 | solution.py:230
  513.4 1.7 subtract_exponential_fusion.6
  520.0 1.7 subtract_exponential_fusion.6
  526.6 1.7 subtract_exponential_fusion.6
  533.2 1.7 subtract_exponential_fusion.6
  539.8 1.7 subtract_exponential_fusion.6
  546.4 1.7 subtract_exponential_fusion.6
  556.1 1.8 multiply_reduce_fusion.26
  560.5 3.0 reshape.707
  563.5 2.3 copy.254
  567.3 2.4 fusion.267
  569.8 48.6 %multiply_reduce_fusion.31 = (f32[512]{0:T(512)S(1)}, f32[512]{0:T(512)S(1)}, f32[512]{0:T(512)S(1)}, f32[512]{0:T(512)S(1)}, f32[512]{0:T(512)S(1)}, /*index=5*/f32[512]{0:T(512)S(1)}, f32[512]{0:T(512)S(1)}, f32[512]{0:T(512)S(1)}) fusion(f32[96,56,512]{2,1,0:T(8,128)} %bitcast.472, f32[96]{0:T(128)S(1)} %copy-done.122, f32[96,56,512]{2,1,0:T(8,128)} %bitcast.469, ...), kind=kLoop, calls=%fused_computation.489 | loop fusion | flops 60551168 | bytes 33276672 | tf_op jit(solution)/shard_map/reduce_sum | solution.py:69
  618.6 5.0 fusion.312
  623.6 7.0 fusion.291
  632.6 1.7 fusion.313
  634.3 61.7 %all-reduce.23 = (f32[128,64]{0,1:T(8,128)}, f32[2,512]{1,0:T(2,128)}, f32[9,512]{1,0:T(8,128)}) all-reduce(f32[128,64]{0,1:T(8,128)S(1)} %fusion.313, f32[2,512]{1,0:T(2,128)S(1)} %pad_maximum_fusion.8, f32[9,512]{1,0:T(8,128)S(1)} %stack.167), channel_id=1, replica_groups=mesh['batch'=16,'heads'=2] {'batch'}, use_global_device_ids=true, to_apply=%region_79.80 | all-reduce | flops 13824 | bytes 110592 | tf_op jit(solution)/shard_map/psum | solution.py:474
  696.0 91.3 %all-reduce.32.cloned.1.call-done = bf16[5376,128]{1,0:T(8,128)(2,1)} async-done(((bf16[5376,128]{1,0:T(8,128)(2,1)}), bf16[5376,128]{1,0:T(8,128)(2,1)}) %all-reduce.32.cloned.1.call-update) | async-done | bytes 1376272 | tf_op jit(solution)/shard_map/psum | solution.py:287
  787.3 2.3 fusion.290
  789.8 116.0 %all-reduce.21 = (f32[2,128]{1,0:T(2,128)}, f32[4,128]{1,0:T(4,128)}, f32[128]{0:T(128)}, f32[3,128]{1,0:T(4,128)}, f32[9,64]{1,0:T(8,128)}, /*index=5*/f32[128]{0:T(128)}, f32[3,128]{1,0:T(4,128)}, f32[9,64]{1,0:T(8,128)}) all-reduce(f32[2,128]{1,0:T(2,128)S(1)} %pad_maximum_fusion.10, ...), channel_id=1, replica_groups=mesh['batch'=16,'heads'=2] {'batch','heads'}, use_global_device_ids=true, to_apply=%region_73.74 | all-reduce | flops 2944 | bytes 23552 | tf_op jit(solution)/shard_map/psum | solution.py:456
  905.8 4.3 fusion.284
  910.1 123.8 %all-reduce.34.cloned.1.call-done = (f32[2048,128]{1,0:T(8,128)}, f32[128,128]{1,0:T(8,128)}, f32[512,128]{1,0:T(8,128)}, f32[128,128]{1,0:T(8,128)}, f32[128,128]{1,0:T(8,128)}) async-done(((f32[2048,128]{1,0:T(8,128)}, f32[128,128]{1,0:T(8,128)}, f32[512,128]{1,0:T(8,128)}, f32[128,128]{1,0:T(8,128)}, f32[128,128]{1,0:T(8,128)}), (f32[2048,128]{1,0:T(8,128)}, f32[128,128]{1,0:T(8,128)}, ...) | async-done | bytes 1507344 | tf_op jit(solution)/shard_map/psum | solution.py:456
  1033.9 2.3 copy.363
  (500 shorter events, 122.9 us)
Async XLA Ops:
  7.2 264.9 %copy-start = (bf16[512,128]{1,0:T(8,128)(2,1)S(1)}, bf16[512,128]{1,0:T(8,128)(2,1)}, u32[]{:S(2)}) copy-start(bf16[512,128]{1,0:T(8,128)(2,1)} %param.53) | copy-start | bytes 393220
  7.2 41.8 %copy-start.46 = (bf16[128,64]{0,1:T(8,128)(2,1)S(1)}, bf16[128,64]{0,1:T(8,128)(2,1)}, u32[]{:S(2)}) copy-start(bf16[128,64]{0,1:T(8,128)(2,1)} %param.38) | copy-start | bytes 49156
  7.2 30.1 %all-gather.4.cloned.1.call-start = ((), (), s32[]{:S(2)}) async-start(), calls=%async_computation.3 | async-start | bytes 2064384 | tf_op jit(solution)/shard_map/all_gather | solution.py:333
  8.0 164.8 %all-gather.6.cloned.1.call-start = ((), (), s32[]{:S(2)}) async-start(), calls=%async_computation.4 | async-start | bytes 2064384 | tf_op jit(solution)/shard_map/all_gather | solution.py:361
  13.7 38.2 %copy-start.73 = (f32[128]{0:T(128)}, f32[128]{0:T(128)S(1)}, u32[]{:S(2)}) copy-start(f32[128]{0:T(128)S(1)} %get-tuple-element.1142) | copy-start | bytes 1540
  109.5 36.3 %copy-start.43 = (bf16[128,128]{1,0:T(8,128)(2,1)S(1)}, bf16[128,128]{1,0:T(8,128)(2,1)}, u32[]{:S(2)}) copy-start(bf16[128,128]{1,0:T(8,128)(2,1)} %param.49) | copy-start | bytes 98308
  109.5 36.3 %copy-start.133 = (f32[128]{0:T(128)S(1)}, f32[128]{0:T(128)}, u32[]{:S(2)}) copy-start(f32[128]{0:T(128)} %get-tuple-element.1133) | copy-start | bytes 1540
  110.4 35.5 %copy-start.23 = (bf16[2688,128]{1,0:T(8,128)(2,1)S(1)}, bf16[2688,128]{1,0:T(8,128)(2,1)}, u32[]{:S(2)}) copy-start(bf16[2688,128]{1,0:T(8,128)(2,1)} %param.33) | copy-start | bytes 2064388
  110.4 38.3 %copy-start.123 = (f32[2,512]{1,0:T(2,128)S(1)}, f32[2,512]{1,0:T(2,128)}, u32[]{:S(2)}) copy-start(f32[2,512]{1,0:T(2,128)} %param.50) | copy-start | bytes 12292
  110.4 38.9 %copy-start.69 = (f32[9,512]{1,0:T(8,128)S(1)}, f32[9,512]{1,0:T(8,128)}, u32[]{:S(2)}) copy-start(f32[9,512]{1,0:T(8,128)} %param.52) | copy-start | bytes 55300
  110.9 68.0 %copy-start.33 = (bf16[128,512]{1,0:T(8,128)(2,1)S(1)}, bf16[128,512]{1,0:T(8,128)(2,1)}, u32[]{:S(2)}) copy-start(bf16[128,512]{1,0:T(8,128)(2,1)} %param.51) | copy-start | bytes 393220
  147.6 151.4 %reduce-scatter.2.cloned.1.call-start = ((), (), s32[]{:S(2)}) async-start(), calls=%async_computation.5 | async-start | bytes 2064384 | tf_op jit(solution)/shard_map/reduce_scatter | solution.py:375
  149.9 41.1 %copy-start.54 = (f32[1,512]{1,0:T(1,128)}, f32[1,512]{1,0:T(1,128)S(1)}, u32[]{:S(2)}) copy-start(f32[1,512]{1,0:T(1,128)S(1)} %get-tuple-element.1122) | copy-start | bytes 6148
  149.9 41.1 %copy-start.56 = (f32[1,512]{1,0:T(1,128)}, f32[1,512]{1,0:T(1,128)S(1)}, u32[]{:S(2)}) copy-start(f32[1,512]{1,0:T(1,128)S(1)} %get-tuple-element.1123) | copy-start | bytes 6148
  149.9 41.1 %copy-start.58 = (f32[1,512]{1,0:T(1,128)}, f32[1,512]{1,0:T(1,128)S(1)}, u32[]{:S(2)}) copy-start(f32[1,512]{1,0:T(1,128)S(1)} %get-tuple-element.1124) | copy-start | bytes 6148
  149.9 41.1 %copy-start.60 = (f32[1,512]{1,0:T(1,128)}, f32[1,512]{1,0:T(1,128)S(1)}, u32[]{:S(2)}) copy-start(f32[1,512]{1,0:T(1,128)S(1)} %get-tuple-element.1125) | copy-start | bytes 6148
  149.9 41.1 %copy-start.62 = (f32[1,512]{1,0:T(1,128)}, f32[1,512]{1,0:T(1,128)S(1)}, u32[]{:S(2)}) copy-start(f32[1,512]{1,0:T(1,128)S(1)} %get-tuple-element.1126) | copy-start | bytes 6148
  149.9 41.1 %copy-start.64 = (f32[1,512]{1,0:T(1,128)}, f32[1,512]{1,0:T(1,128)S(1)}, u32[]{:S(2)}) copy-start(f32[1,512]{1,0:T(1,128)S(1)} %get-tuple-element.1127) | copy-start | bytes 6148
  174.6 235.9 %copy-start.34 = (f32[5376]{0:T(1024)}, f32[5376]{0:T(1024)S(1)}, u32[]{:S(2)}) copy-start(f32[5376]{0:T(1024)S(1)} %broadcast_multiply_fusion.8) | copy-start | bytes 64516
  178.8 231.7 %copy-start.36 = (f32[5376]{0:T(1024)}, f32[5376]{0:T(1024)S(1)}, u32[]{:S(2)}) copy-start(f32[5376]{0:T(1024)S(1)} %add_rsqrt_fusion.4) | copy-start | bytes 64516
  191.0 51.0 %copy-start.78 = (f32[1,512]{1,0:T(1,128)S(1)}, f32[1,512]{1,0:T(1,128)}, u32[]{:S(2)}) copy-start(f32[1,512]{1,0:T(1,128)} %get-tuple-element.1131) | copy-start | bytes 6148
  272.1 26.8 %copy-start.20 = (f32[2688,128]{1,0:T(8,128)S(1)}, f32[2688,128]{1,0:T(8,128)}, u32[]{:S(2)}) copy-start(f32[2688,128]{1,0:T(8,128)} %get-tuple-element.1141) | copy-start | bytes 4128772
  272.1 26.8 %copy-start.32 = (bf16[2688,128]{1,0:T(8,128)(2,1)S(1)}, bf16[2688,128]{1,0:T(8,128)(2,1)}, u32[]{:S(2)}) copy-start(bf16[2688,128]{1,0:T(8,128)(2,1)} %param.35) | copy-start | bytes 2064388
  272.1 26.8 %copy-start.148 = (f32[128]{0:T(128)S(1)}, f32[128]{0:T(128)}, u32[]{:S(2)}) copy-start(f32[128]{0:T(128)} %get-tuple-element.1132) | copy-start | bytes 1540
  274.8 52.4 %all-gather.8.cloned.1.call-start = ((), (), s32[]{:S(2)}) async-start(), calls=%async_computation.6 | async-start | bytes 2064384 | tf_op jit(solution)/shard_map/all_gather | solution.py:379
  302.1 155.8 %all-reduce.30.cloned.1.call-start = ((), (), s32[]{:S(2)}) async-start(), calls=%async_computation.7 | async-start | bytes 2752512 | tf_op jit(solution)/shard_map/psum | solution.py:287
  410.5 47.4 %copy-start.67 = (f32[128]{0:T(128)S(1)}, f32[128]{0:T(128)}, u32[]{:S(2)}) copy-start(f32[128]{0:T(128)} %get-tuple-element.1143) | copy-start | bytes 1540
  410.5 50.3 %copy-start.19 = (bf16[2688,128]{1,0:T(8,128)(2,1)S(1)}, bf16[2688,128]{1,0:T(8,128)(2,1)}, u32[]{:S(2)}) copy-start(bf16[2688,128]{1,0:T(8,128)(2,1)} %get-tuple-element.993) | copy-start | bytes 2064388
  410.6 55.3 %copy-start.44 = (bf16[128,128]{1,0:T(8,128)(2,1)S(1)}, bf16[128,128]{1,0:T(8,128)(2,1)}, u32[]{:S(2)}) copy-start(bf16[128,128]{1,0:T(8,128)(2,1)} %param.49) | copy-start | bytes 98308
  460.8 21.0 %copy-start.49 = (bf16[128,128]{1,0:T(8,128)(2,1)S(1)}, bf16[128,128]{1,0:T(8,128)(2,1)}, u32[]{:S(2)}) copy-start(bf16[128,128]{1,0:T(8,128)(2,1)} %param.47) | copy-start | bytes 98308
  460.8 21.0 %copy-start.71 = (f32[9,64]{1,0:T(8,128)S(1)}, f32[9,64]{1,0:T(8,128)}, u32[]{:S(2)}) copy-start(f32[9,64]{1,0:T(8,128)} %param.48) | copy-start | bytes 6916
  460.8 21.0 %copy-start.84 = (f32[3,128]{1,0:T(4,128)S(1)}, f32[3,128]{1,0:T(4,128)}, u32[]{:S(2)}) copy-start(f32[3,128]{1,0:T(4,128)} %param.46) | copy-start | bytes 4612
  460.8 21.0 %copy-start.124 = (f32[128]{0:T(128)S(1)}, f32[128]{0:T(128)}, u32[]{:S(2)}) copy-start(f32[128]{0:T(128)} %param.45) | copy-start | bytes 1540
  467.4 13.5 %all-to-all-start.1 = ((bf16[2688,2,64]{0,2,1:T(8,128)(2,1)}), bf16[2688,2,64]{0,2,1:T(8,128)(2,1)S(1)}, u32[]{:S(2)}, u32[]{:S(2)}) async-start(bf16[2688,2,64]{0,2,1:T(8,128)(2,1)} %bitcast.130), calls=%async_computation.2 | async-start | bytes 1376256 | tf_op jit(solution)/shard_map/all_to_all | solution.py:400
  470.9 316.4 %all-reduce.32.cloned.1.call-start = ((), (), s32[]{:S(2)}) async-start(), calls=%async_computation.8 | async-start | bytes 2752512 | tf_op jit(solution)/shard_map/psum | solution.py:287
  493.6 17.2 %copy-start.144 = (f32[128]{0:T(128)}, f32[128]{0:T(128)S(1)}, u32[]{:S(2)}) copy-start(f32[128]{0:T(128)S(1)} %get-tuple-element.1100) | copy-start | bytes 1540 | tf_op jit(solution)/shard_map/conditional.1
  493.8 17.0 %copy-start.86 = (f32[64]{0:T(128)}, f32[64]{0:T(128)S(1)}, u32[]{:S(2)}) copy-start(f32[64]{0:T(128)S(1)} %get-tuple-element.1108) | copy-start | bytes 772 | tf_op jit(solution)/shard_map/conditional.1
  493.8 17.0 %copy-start.88 = (f32[64]{0:T(128)}, f32[64]{0:T(128)S(1)}, u32[]{:S(2)}) copy-start(f32[64]{0:T(128)S(1)} %get-tuple-element.1109) | copy-start | bytes 772 | tf_op jit(solution)/shard_map/conditional.1
  493.8 17.0 %copy-start.90 = (f32[64]{0:T(128)}, f32[64]{0:T(128)S(1)}, u32[]{:S(2)}) copy-start(f32[64]{0:T(128)S(1)} %get-tuple-element.1110) | copy-start | bytes 772 | tf_op jit(solution)/shard_map/conditional.1
  493.8 17.0 %copy-start.91 = (f32[64]{0:T(128)}, f32[64]{0:T(128)S(1)}, u32[]{:S(2)}) copy-start(f32[64]{0:T(128)S(1)} %get-tuple-element.1111) | copy-start | bytes 772 | tf_op jit(solution)/shard_map/conditional.1
  493.8 17.0 %copy-start.92 = (f32[64]{0:T(128)}, f32[64]{0:T(128)S(1)}, u32[]{:S(2)}) copy-start(f32[64]{0:T(128)S(1)} %get-tuple-element.1112) | copy-start | bytes 772 | tf_op jit(solution)/shard_map/conditional.1
  493.8 17.0 %copy-start.93 = (f32[64]{0:T(128)}, f32[64]{0:T(128)S(1)}, u32[]{:S(2)}) copy-start(f32[64]{0:T(128)S(1)} %get-tuple-element.1113) | copy-start | bytes 772 | tf_op jit(solution)/shard_map/conditional.1
  493.8 17.0 %copy-start.94 = (f32[64]{0:T(128)}, f32[64]{0:T(128)S(1)}, u32[]{:S(2)}) copy-start(f32[64]{0:T(128)S(1)} %get-tuple-element.1114) | copy-start | bytes 772 | tf_op jit(solution)/shard_map/conditional.1
  493.8 17.0 %copy-start.95 = (f32[64]{0:T(128)}, f32[64]{0:T(128)S(1)}, u32[]{:S(2)}) copy-start(f32[64]{0:T(128)S(1)} %get-tuple-element.1115) | copy-start | bytes 772 | tf_op jit(solution)/shard_map/conditional.1
  512.1 41.9 %copy-start.87 = (f32[64]{0:T(128)S(1)}, f32[64]{0:T(128)}, u32[]{:S(2)}) copy-start(f32[64]{0:T(128)} %copy-done.86) | copy-start | bytes 772 | tf_op jit(solution)/shard_map/conditional.1
  512.2 41.9 %copy-start.89 = (f32[64]{0:T(128)S(1)}, f32[64]{0:T(128)}, u32[]{:S(2)}) copy-start(f32[64]{0:T(128)} %copy-done.88) | copy-start | bytes 772 | tf_op jit(solution)/shard_map/conditional.1
  566.0 52.4 %copy-start.47 = (f32[128,128]{1,0:T(8,128)}, f32[128,128]{1,0:T(8,128)S(1)}, u32[]{:S(2)}) copy-start(f32[128,128]{1,0:T(8,128)S(1)} %get-tuple-element.411) | copy-start | bytes 196612
  566.0 52.4 %copy-start.81 = (f32[3,128]{1,0:T(4,128)}, f32[3,128]{1,0:T(4,128)S(1)}, u32[]{:S(2)}) copy-start(f32[3,128]{1,0:T(4,128)S(1)} %get-tuple-element.405) | copy-start | bytes 4612
  569.7 48.8 %copy-start.76 = (f32[512]{0:T(512)S(1)}, f32[512]{0:T(512)}, u32[]{:S(2)}) copy-start(f32[512]{0:T(512)} %get-tuple-element.877) | copy-start | bytes 6148
  569.7 48.8 %copy-start.77 = (f32[512]{0:T(512)S(1)}, f32[512]{0:T(512)}, u32[]{:S(2)}) copy-start(f32[512]{0:T(512)} %get-tuple-element.1116) | copy-start | bytes 6148
  569.7 48.8 %copy-start.26 = (bf16[5376,128]{1,0:T(8,128)(2,1)S(1)}, bf16[5376,128]{1,0:T(8,128)(2,1)}, u32[]{:S(2)}) copy-start(bf16[5376,128]{1,0:T(8,128)(2,1)} %all-gather.8.cloned.1.call-done) | copy-start | bytes 4128772
  569.7 340.4 %all-reduce.36.cloned.1.call-start = ((), (), s32[]{:S(2)}) async-start(), calls=%async_computation.10 | async-start | bytes 1048576 | tf_op jit(solution)/shard_map/psum | solution.py:474
  630.6 156.8 %copy-start.74 = (f32[128]{0:T(128)S(1)}, f32[128]{0:T(128)}, u32[]{:S(2)}) copy-start(f32[128]{0:T(128)} %copy-done.73) | copy-start | bytes 1540
  630.6 159.1 %copy-start.145 = (f32[128]{0:T(128)S(1)}, f32[128]{0:T(128)}, u32[]{:S(2)}) copy-start(f32[128]{0:T(128)} %get-tuple-element.885) | copy-start | bytes 1540
  630.6 159.1 %copy-start.146 = (f32[128]{0:T(128)S(1)}, f32[128]{0:T(128)}, u32[]{:S(2)}) copy-start(f32[128]{0:T(128)} %get-tuple-element.990) | copy-start | bytes 1540
  630.6 159.1 %copy-start.149 = (f32[128]{0:T(128)S(1)}, f32[128]{0:T(128)}, u32[]{:S(2)}) copy-start(f32[128]{0:T(128)} %get-tuple-element.992) | copy-start | bytes 1540
  630.6 159.2 %copy-start.143 = (f32[128]{0:T(128)S(1)}, f32[128]{0:T(128)}, u32[]{:S(2)}) copy-start(f32[128]{0:T(128)} %get-tuple-element.880) | copy-start | bytes 1540
  630.6 159.2 %copy-start.80 = (f32[3,128]{1,0:T(4,128)S(1)}, f32[3,128]{1,0:T(4,128)}, u32[]{:S(2)}) copy-start(f32[3,128]{1,0:T(4,128)} %copy-done.79) | copy-start | bytes 4612
  630.6 159.2 %copy-start.82 = (f32[3,128]{1,0:T(4,128)S(1)}, f32[3,128]{1,0:T(4,128)}, u32[]{:S(2)}) copy-start(f32[3,128]{1,0:T(4,128)} %copy-done.81) | copy-start | bytes 4612
  630.6 159.2 %copy-start.153 = (f32[128]{0:T(128)S(1)}, f32[128]{0:T(128)}, u32[]{:S(2)}) copy-start(f32[128]{0:T(128)} %copy-done.152) | copy-start | bytes 1540
  630.6 159.2 %copy-start.156 = (f32[128]{0:T(128)S(1)}, f32[128]{0:T(128)}, u32[]{:S(2)}) copy-start(f32[128]{0:T(128)} %copy-done.155) | copy-start | bytes 1540
  630.6 275.1 %copy-start.48 = (f32[2688]{0:T(1024)S(1)}, f32[2688]{0:T(1024)}, u32[]{:S(2)}) copy-start(f32[2688]{0:T(1024)} %dynamic-slice.11) | copy-start | bytes 32260
  630.7 403.2 %all-reduce.34.cloned.1.call-start = ((), (), s32[]{:S(2)}) async-start(), calls=%async_computation.9 | async-start | bytes 3014656 | tf_op jit(solution)/shard_map/psum | solution.py:456
  787.3 258.3 %copy-start.1 = (bf16[512,128]{1,0:T(8,128)(2,1)S(1)}, bf16[512,128]{1,0:T(8,128)(2,1)}, u32[]{:S(2)}) copy-start(bf16[512,128]{1,0:T(8,128)(2,1)} %param.53) | copy-start | bytes 393220
  (61 other events, 320.6 us)
Sparse Core Ops, SparseCore 0:
  9.6 27.7 all-gather.3
  147.7 25.0 all-gather.5
  275.0 23.9 reduce-scatter.1
  302.2 24.9 all-gather.7
  410.7 47.1 all-reduce.29
  569.8 217.4 all-reduce.31
  792.3 99.2 all-reduce.35
  900.4 133.4 all-reduce.33
where the time goes:
time: 1060 us; the launch traced here: 1050 us
  waiting for transfers between devices  364 us (34%)
  other arithmetic  251 us (24%)
  blocking collectives  212 us (20%)
  local copies, waits for them, and re-layouts  102 us (10%)
  matrix products  87.1 us (8%)
  loops' own time  17.2 us (2%)
  between operations  15.4 us (1%)
    psum x2, waiting for transfers between devices, norm_sum(): lax.psum(partial_grad.astype(jnp.bfloat16), 'heads').astype(jnp.float32)  135 us
    psum x1, waiting for transfers between devices, per_device(): lax.psum((front_gains_grad, front_shifts_grad, proj_grad, coarse_conv_gra...  124 us
    psum x1, blocking collectives, per_device(): lax.psum((front_gains_grad, front_shifts_grad, proj_grad, coarse_conv_gra...  116 us
    add x4, other arithmetic, depthwise_ext(): result + padded[above:above + grid_rows, across:across + grid_cols] * tap...  101 us
    reduce_sum x4, other arithmetic, tap_grads_ext(): collected.append(jnp.sum(shifted * grad_grid * same_image, axis=(0, 1)))  62.8 us
    psum x1, blocking collectives, per_device(): lax.psum((query_w_grad, hidden_shift_grad, fc1_grad, depth_grad, fc2_grad...  61.7 us
    all_to_all x1, blocking collectives, per_device(): lax.all_to_all(heads_own_b, 'heads', split_axis=0, concat_axis=1, tiled=T...  34 us
    convert_element_type x1, other arithmetic, per_device(): activated = gelu_value(spread).astype(jnp.bfloat16)  27.8 us
  transfers between devices with their start and end apart: 9, of which 8 were waited for; matrix products, arithmetic and copies ran while one was open for 8% of the time, Pallas kernels for 0%

commit v1 on v0

v1 whole, which is shorter than its diff:
```python
import functools

import jax
import jax.numpy as jnp
from jax import lax
from jax.experimental import pallas as pl
from jax.experimental.pallas import tpu as pltpu
from jax.sharding import PartitionSpec as P

W = 56
BAND = 4 * W
SLOTS = 256
COARSE = 16
FINE = 64
CELLS = COARSE + FINE
MAX_BANDS = 14
EPS = 1e-06
F32 = jnp.float32
BF16 = jnp.bfloat16
SCALE = 32**-0.5
LOG2E = 1.4426950408889634
ROOT = 0.7071067811865476
EXP_SCALE = SCALE * LOG2E
BIG = -1e9
MIB = 1024 * 1024
STEP = 256
SPAN = 512
MESH = pl.DeviceIdType.MESH
TAPS = 9
KEPT = TAPS * 128 + 16
WIDE = (TAPS + 1) * 128
QUARTER = 768
CONV = 512
REST = QUARTER - CONV
SMALL = 48
SPLIT = 544


def dot(left, right):
    return jnp.dot(left, right, preferred_element_type=F32)


def dot_t(left, right):
    return lax.dot_general(left, right, (((1,), (1,)), ((), ())), preferred_element_type=F32)


def dot_in(left, right):
    return lax.dot_general(left, right, (((0,), (0,)), ((), ())), preferred_element_type=F32)


def gauss(values):
    return 0.5 + 0.5 * lax.erf(values * ROOT), jnp.exp2(values * values * (-0.5 * LOG2E))


def gelu_slope(values, cdf, bell):
    return cdf + values * bell * 0.3989422804014327


def fold_rows(values):
    wide = jnp.sum(values.reshape(-1, 64, 128), axis=0)
    return jnp.sum(wide.reshape(8, 8, 128), axis=0)


def norm_hat(values):
    centred = values - jnp.mean(values, axis=-1, keepdims=True)
    inverse = lax.rsqrt(jnp.mean(centred * centred, axis=-1, keepdims=True) + EPS)
    return centred * inverse, inverse


def norm_back(grad_scaled, hat, inverse):
    centre = jnp.mean(grad_scaled, axis=-1, keepdims=True)
    along = jnp.mean(grad_scaled * hat, axis=-1, keepdims=True)
    return inverse * (grad_scaled - centre - hat * along)


def slot_map(slot, token):
    a, b, c = slot >> 6, (slot >> 4) & 3, slot & 15
    hit = (token == a * W + 4 * c + b) & (c < 14)
    return jnp.where(hit, 1.0, 0.0).astype(BF16)


def to_slots():
    shape = (SLOTS, BAND)
    return slot_map(
        lax.broadcasted_iota(jnp.int32, shape, 0), lax.broadcasted_iota(jnp.int32, shape, 1)
    )


def from_slots():
    shape = (BAND, SLOTS)
    return slot_map(
        lax.broadcasted_iota(jnp.int32, shape, 1), lax.broadcasted_iota(jnp.int32, shape, 0)
    )


def cell_valid(shape, axis):
    return (lax.broadcasted_iota(jnp.int32, shape, axis) & 15) < 14


def roll_cells(values, step):
    lead = values.shape[:-2]
    flat = values.reshape(-1, values.shape[-1])
    flat = pltpu.roll(flat, step % flat.shape[0], 0)
    return flat.reshape(lead + values.shape[-2:])


def by_band(values, mask):
    count = values.shape[0]
    wide = values.reshape(count, -1, 8, 128) * mask.reshape(count, 1, 8, 128)
    return wide.reshape(values.shape)


def row_taps(taps, flip):
    order = [8 - i for i in range(9)] if flip else list(range(9))
    return [taps[i : i + 1, :] for i in order]


def depthwise_coarse(ext, above, below, taps, flip=False):
    t = row_taps(taps, flip)
    up, mid, down = by_band(ext[:-2], above), ext[1:-1], by_band(ext[2:], below)
    left, centre, right = (up * t[b] + mid * t[3 + b] + down * t[6 + b] for b in range(3))
    return centre + roll_cells(left, 1) + roll_cells(right, -1)


def fine_rows(ext, above, below):
    bands = ext.shape[0] - 2
    grid = ext.reshape(bands + 2, 2, 2, 16, 128)
    first, second = grid[:, 0], grid[:, 1]
    up = (by_band(second[:-2], above), first[1:-1])
    mid = (first[1:-1], second[1:-1])
    down = (second[1:-1], by_band(first[2:], below))
    return up, mid, down


def depthwise_fine(ext, above, below, taps, flip=False):
    t = row_taps(taps, flip)
    ups, mids, downs = fine_rows(ext, above, below)
    rows = []
    for up, mid, down in zip(ups, mids, downs):
        left, centre, right = (up * t[b] + mid * t[3 + b] + down * t[6 + b] for b in range(3))
        even = centre[:, 0] + roll_cells(left[:, 1], 1) + right[:, 1]
        odd = centre[:, 1] + left[:, 0] + roll_cells(right[:, 0], -1)
        rows.append((even, odd))
    return rows


def greet(*peers):
    barrier = pltpu.get_barrier_semaphore()
    for peer in peers:
        pl.semaphore_signal(barrier, inc=1, device_id=peer, device_id_type=MESH)


def met(count):
    pl.semaphore_wait(pltpu.get_barrier_semaphore(), count)


def fetch(pairs, sems):
    loads = [pltpu.make_async_copy(source, target, sems.at[i]) for i, (source, target) in enumerate(pairs)]
    for load in loads:
        load.start()
    return loads


def link(source, target, send_sem, recv_sem, peer):
    return pltpu.make_async_remote_copy(
        src_ref=source,
        dst_ref=target,
        send_sem=send_sem,
        recv_sem=recv_sem,
        device_id=peer,
        device_id_type=MESH,
    )


def remote(source, target, send_sem, recv_sem, peer):
    made = link(source, target, send_sem, recv_sem, peer)
    made.start()
    return made


def across():
    return (lax.axis_index("batch"), 1 - lax.axis_index("heads"))


def swap_lanes(values):
    half = values.shape[1] // 2
    return jnp.concatenate([values[:, half:], values[:, :half]], axis=1)


def keep_lanes(values, upper):
    lane = lax.broadcasted_iota(jnp.int32, values.shape, 1)
    return jnp.where((lane >= 64) if upper else (lane < 64), values, 0.0)


def pad_taps(taps, upper):
    gap = jnp.zeros(taps.shape, F32)
    return jnp.concatenate([gap, taps] if upper else [taps, gap], axis=1)


def band_tables(heights, table, meta, total):
    count = heights.shape[1]
    number = jnp.int32(0)
    start = jnp.int32(0)
    end = heights[0, 0]
    last = jnp.int32(-2)
    images, sames = [], []
    for band in range(total):
        passed = band >= end
        number = jnp.where(passed, number + 1, number)
        start = jnp.where(passed, end, start)
        grown = heights[0, jnp.minimum(number, count - 1)]
        grown = jnp.where(number < count, grown, 0)
        end = jnp.where(passed, end + grown, end)
        image = jnp.where(band < end, number, -1)
        same = jnp.where(image == last, 1, 0)
        last = image
        table[0, band] = image
        table[1, band] = jnp.minimum(start, total - MAX_BANDS)
        table[2, band] = same
        images.append(image)
        sames.append(same)
    for band in range(total, table.shape[1]):
        for row in range(3):
            table[row, band] = jnp.int32(0)
    sames.append(jnp.int32(0))
    for band in range(total):
        for row, value in enumerate((sames[band], sames[band + 1], images[band])):
            meta[row, band] = jnp.full((8, 128), value.astype(F32), F32)


def front_kernel(
    heights, tok, gains, shifts, conv_c, gain_c, shifts_c, kv_c, conv_f, gain_f, shifts_f, kv_f,
    query_t,
    table, meta, xn_out, hat_out, red_c, red_f, slab, other, query_o,
    send, send_sems, recv_sems,
):
    bands = xn_out.shape[0]
    peer = across()
    greet(peer)
    copies = []

    def give(source, target):
        at = len(copies)
        copies.append(remote(source, target, send_sems.at[at], recv_sems.at[at], peer))

    place = to_slots()

    def one_band(band, carry):
        values = tok[pl.ds(pl.multiple_of(band * BAND, 16), BAND), :].astype(F32)
        hat, _ = norm_hat(values)
        normed = (hat * gains[0:1, :] + shifts[0:1, :]).astype(BF16)
        both = dot(place, jnp.concatenate([normed, hat.astype(BF16)], axis=1)).astype(BF16)
        xn_out[band] = both[:, :128]
        hat_out[band] = both[:, 128:]
        return carry

    def reduce(patches, conv, gain, shift, kv, out, at):
        red = dot(patches, conv) + shift[0:1, :]
        out[at : at + red.shape[0], :] = red
        hat, _ = norm_hat(red)
        normed = hat * gain[...] + shift[1:2, :]
        cdf, _ = gauss(normed)
        return dot((normed * cdf).astype(BF16), kv)

    kv_f_sw = swap_lanes(kv_f[...])
    part = bands // 2
    for first in (0, part):
        lax.fori_loop(first, first + part, one_band, 0, unroll=2)
        grid = xn_out[first : first + part].reshape(part, 16, 16, 128)
        patches = jnp.concatenate([fine_patch(grid, i) for i in range(4)], axis=1)
        pair = reduce(patches, conv_f[...], gain_f, shifts_f, kv_f_sw, red_f, first * FINE)
        pair = pair + keep_lanes(shifts_f[2:3, :], False)
        pair = jnp.where(cell_valid(pair.shape, 0), pair, 0.0).reshape(part, FINE, 128)
        slab[first : first + part, COARSE:CELLS, :] = pair
        send[first : first + part, COARSE:CELLS, :] = pair.astype(BF16)
        here = (pl.ds(first, part), pl.ds(COARSE, FINE))
        if first == 0:
            met(1)
        give(send.at[here], other.at[here])
        if first == 0:
            give(query_t, query_o)
    grid = xn_out[...].reshape(bands, 16, 16, 128)
    patches = jnp.concatenate([grid[:, i].reshape(bands * 16, 128) for i in range(16)], axis=1)
    pair = reduce(patches, conv_c[...], gain_c, shifts_c, kv_c[...], red_c, 0)
    pair = pair + keep_lanes(swap_lanes(shifts_c[2:3, :]), True)
    pair = jnp.where(cell_valid(pair.shape, 0), pair, 0.0).reshape(bands, COARSE, 128)
    slab[:, 0:COARSE, :] = pair
    send[:, 0:COARSE, :] = pair.astype(BF16)
    here = pl.ds(0, COARSE)
    give(send.at[:, here], other.at[:, here])
    band_tables(heights, table, meta, 2 * bands)
    for made in copies:
        made.wait()


def fine_slot(part, row, column):
    return (2 * row + (part >> 1)) * 4 + 2 * column + (part & 1)


def fine_patch(grid, part):
    bands = grid.shape[0]
    blocks = [
        grid[:, fine_slot(part, row, column)].reshape(bands, 1, 16, 128)
        for row in range(2)
        for column in range(2)
    ]
    return jnp.concatenate(blocks, axis=1).reshape(bands * FINE, 128)


def head_lanes(values, head):
    lane = lax.broadcasted_iota(jnp.int32, values.shape, 1)
    return jnp.where((lane >> 5) == head, values, jnp.zeros((), BF16))


def head_rows(values, head):
    row = lax.broadcasted_iota(jnp.int32, values.shape, 0)
    return jnp.where((row >> 5) == head, values, jnp.zeros((), BF16))


def score_rows(query_t, head, image, fine):
    row = lax.broadcasted_iota(jnp.int32, query_t.shape, 0)
    tag = row if fine else row - 64
    fill = jnp.where((tag >= 0) & (tag <= NOBODY) & (tag != image), BIG, 0.0).astype(BF16)
    return jnp.where((row >> 5) == head, query_t, fill)


def with_offset(rows, at, offset):
    start = at // 16 * 16
    block = rows[start : start + 16]
    row = lax.broadcasted_iota(jnp.int32, block.shape, 0)
    for i in range(3):
        term = offset.astype(BF16)
        block = jnp.where(row == at - start + i, term, block)
        offset = offset - term.astype(F32)
    parts = [rows[:start]] if start else []
    return jnp.concatenate(parts + [block, rows[start + 16 :]], axis=0)


def full_query(query_t, query_o, side):
    own, other = query_t[...].astype(F32), query_o[...].astype(F32)
    return jnp.where(
        side == 0,
        jnp.concatenate([own, other], axis=0),
        jnp.concatenate([other, own], axis=0),
    )


def window(ref, first):
    part = ref[pl.ds(first, MAX_BANDS)]
    return part.reshape(-1, 128).astype(BF16)


PACKED = 56
CHUNKS = ((0, 224), (224, 224), (448, 224), (672, 112))
HALVES = ((0, 8), (8, 6))
NOBODY = 32
ONES = 40


def tree_max(values):
    count = values.shape[0]
    while count % 16 == 0:
        count //= 2
        values = jnp.maximum(values[:count], values[count:])
    return jnp.max(values, axis=0, keepdims=True)


def attend_kernel(
    table, slab, other, meta, taps_c, taps_f, shifts_c, shifts_f, xn, tok, query_t, query_o, proj_w,
    gains, shifts, fc1, fc2, depth, hidden, cot,
    x1_out, xm_out, o_out, ot_out, lse_out, key_c, key_f, val_c, val_f, fc1_o, fc2_o, depth_o,
    hidden_o, cot_o,
    grid_ref, query_ref, place_ref, send_sems, recv_sems,
):
    step = pl.program_id(0)
    bands = slab.shape[0]
    total = 2 * bands
    side = lax.axis_index("heads")
    peer = across()
    halo = 2 * W
    edge = pl.multiple_of((1 - side) * (cot.shape[0] - halo), 16)
    swaps = [
        link(source, target, send_sems.at[i], recv_sems.at[i], peer)
        for i, (source, target) in enumerate(
            (
                (cot.at[pl.ds(edge, halo)], cot_o),
                (depth, depth_o),
                (hidden, hidden_o),
                (fc1, fc1_o),
                (fc2, fc2_o),
            )
        )
    ]

    @pl.when(step == 0)
    def _():
        greet(peer)
        place_ref[...] = from_slots()
        query_ref[...] = full_query(query_t, query_o, side).T.astype(BF16)
        grid_ref[0] = jnp.zeros((CELLS, 128), F32)
        grid_ref[total + 1] = jnp.zeros((CELLS, 128), F32)
        grid_ref[pl.ds(1 + side * bands, bands)] = slab[...]
        grid_ref[pl.ds(1 + (1 - side) * bands, bands)] = other[...].astype(F32)
        above, below, image = meta[0], meta[1], meta[2]
        lane = lax.broadcasted_iota(jnp.int32, (total, 16, 128), 2).astype(F32)
        valid = cell_valid((total, 16, 128), 1)
        wide = jnp.broadcast_to(image.reshape(total, 1, 8, 128), (total, 2, 8, 128))
        wide = wide.reshape(total, 16, 128)
        mark = jnp.where(valid & (wide >= 0.0), wide, float(NOBODY))

        ext = grid_ref[:, 0:COARSE, :]
        own = ext[1:-1]
        local = keep_lanes(shifts_c[2:3, :], True)
        mixed = own + depthwise_coarse(ext, above, below, pad_taps(taps_c[...], True)) + local
        val_c[...] = jnp.where(lane < 3.0, 1.0, mixed).astype(BF16)
        place = lane - 64.0
        one = (place >= ONES) & (place < ONES + 3)
        tag = jnp.where((place == mark) | one, 1.0, 0.0)
        keys = jnp.where(lane < 64.0, own, tag)
        key_c[...] = keys.astype(BF16)

        ext = grid_ref[:, COARSE:CELLS, :]
        local = keep_lanes(swap_lanes(shifts_f[2:3, :]), False)
        rows = depthwise_fine(ext, above, below, pad_taps(taps_f[...], False))
        tag = jnp.where((lane == mark) | ((lane >= ONES) & (lane < ONES + 3)), 1.0, 0.0)
        one = (lane >= 64.0) & (lane < 67.0)
        for row in range(2):
            for column in range(2):
                at = (2 * row + column) * 16
                own = ext[1:-1, at : at + 16, :]
                mixed = own + rows[row][column] + local
                cell = (2 * row + column) * 14
                val_f[:, cell : cell + 14, :] = jnp.where(one, 1.0, mixed)[:, 0:14]
                keys = jnp.where(lane >= 64.0, own.astype(BF16).astype(F32), tag)
                key_f[:, cell : cell + 14, :] = keys[:, 0:14]
        met(1)
        for swap in swaps:
            swap.start()

    each = xn.shape[0]
    images = [table[0, side * bands + each * step + i] for i in range(each)]
    firsts = [table[1, side * bands + each * step + i] for i in range(each)]
    queries = [
        dot(xn[i], query_ref[...]).astype(BF16).astype(F32).T.astype(BF16) for i in range(each)
    ]
    turned, windows = {}, {}

    def score(unit):
        i, head, part = unit
        fine = head >= 2
        start, size = CHUNKS[part]
        rows = slice(start, start + size)
        if not head & 1:
            if part == 0:
                windows[i, fine] = [
                    window(ref, firsts[i]) for ref in ((key_f, val_f) if fine else (key_c, val_c))
                ]
            turned[i, fine, part] = windows[i, fine][1][rows].T
        keys = windows[i, fine][0][rows]
        return dot(keys, score_rows(queries[i], head, images[i], fine))

    outs = [[None] * 4 for _ in range(each)]
    mixed = {}
    lse_out[...] = jnp.zeros(lse_out.shape, F32)

    def mix(unit, scores):
        i, head, part = unit
        fine = head >= 2
        top = tree_max(scores) * EXP_SCALE
        expo = jnp.exp2(scores * EXP_SCALE - top).astype(BF16)
        row = 32 * (head & 1) + (0 if fine else 64)
        vals = turned[i, fine, part][row : row + 32]
        left = jnp.concatenate([vals, jnp.ones((16, CHUNKS[part][1]), BF16)], axis=0)
        done = mixed.setdefault((i, head), [])
        done.append((top, dot(left, expo)))
        if len(done) < (4 if fine else 1):
            return
        top = functools.reduce(jnp.maximum, [part_top for part_top, _ in done])
        total = None
        for part_top, value in done:
            value = value * jnp.exp2(part_top - top)
            total = value if total is None else total + value
        sums = total[32:33]
        lse_out[i, head : head + 1, :] = top + jnp.log2(sums)
        outs[i][head] = total[0:32] * (1.0 / sums)

    waiting = []
    for i in range(each):
        for head, parts in ((2, 4), (0, 1), (3, 4), (1, 1)):
            for part in range(parts):
                waiting.append(((i, head, part), score((i, head, part))))
                if len(waiting) > 6:
                    mix(*waiting.pop(0))
    for unit, scores in waiting:
        mix(unit, scores)
    place = place_ref[...]
    for i in range(each):
        live = jnp.where(images[i] >= 0, 1.0, 0.0)
        out_t = jnp.concatenate(outs[i], axis=0) * live
        ot_out[i] = out_t
        heads_out = dot(place, out_t.T.astype(BF16)).astype(BF16)
        at = slice(i * BAND, (i + 1) * BAND)
        o_out[at, :] = heads_out
        middle = tok[at, :].astype(F32) + dot(heads_out, proj_w[...]) + shifts[1:2, :]
        x1_out[at, :] = middle
        hat, _ = norm_hat(middle)
        xm_out[at, :] = (hat * gains[1:2, :] + shifts[2:3, :]).astype(BF16)

    @pl.when(step == pl.num_programs(0) - 1)
    def _():
        for swap in swaps:
            swap.wait()


def shift_right(values):
    column = lax.broadcasted_iota(jnp.int32, values.shape, 0)
    return jnp.where(column == 0, 0.0, pltpu.roll(values, 1, 0))


def shift_left(values):
    column = lax.broadcasted_iota(jnp.int32, values.shape, 0)
    return jnp.where(column == W - 1, 0.0, pltpu.roll(values, W - 1, 0))


def mask_lanes():
    lane = lax.broadcasted_iota(jnp.int32, (W, 128), 1)
    column = lax.broadcasted_iota(jnp.int32, (W, 128), 0)
    tap = jnp.where(lane < 32, lane & 15, 15)
    parts = []
    for a in range(3):
        hit = tap == 3 * a + 1
        hit = hit | ((tap == 3 * a) & (column > 0)) | ((tap == 3 * a + 2) & (column < W - 1))
        if a == 1:
            hit = hit | (tap == TAPS)
        parts.append(jnp.where(hit, 1.0, 0.0))
    return parts


def hidden_kernel(
    table, x1_in, xm, cot, cot_o, heads_in, fc1, fc1_o, fc2, fc2_o, depth, depth_o, hidden, hidden_o,
    gains, shifts, proj_w,
    out, dx1_out, do_out, split_g, mid_g,
    xm_ext, halo_ref, moved, wide, wide_t, weights, weights_t, taps, bias, base_ref, fc2_t, dy, dy_t, act, du,
    sums, dxm, out_acc, x1, heads_out, send_sem, recv_sem, load_sems,
):
    side = lax.axis_index("heads")
    peer = across()
    tokens = x1.shape[0]
    rows = tokens // W
    bands = tokens // BAND
    halo = 2 * W
    extra = wide.shape[0] - tokens
    mine = fc1.shape[1]
    width = 2 * mine
    halo_at = pl.multiple_of((1 - side) * (halo + tokens), 16)
    halo_row = 1 + (1 - side) * (rows + 1)
    greet(peer)
    loads = fetch(((x1_in, x1), (heads_in, heads_out)), load_sems)
    edge = pl.multiple_of((1 - side) * (tokens - halo), 16)
    swap = link(xm.at[pl.ds(edge, halo)], halo_ref, send_sem, recv_sem, peer)

    def live_band(band):
        return jnp.where(table[0, band] >= 0, 1.0, 0.0)

    def neighbour(row):
        place = side * rows - 2 + row
        band = jnp.maximum(place, 0) >> 2
        up = jnp.where((place & 3) == 0, table[2, band], 1)
        down = jnp.where((place & 3) == 3, table[2, band + 1], 1)
        return up.astype(F32), down.astype(F32)

    xm_ext[0:halo, :] = jnp.zeros((halo, 128), BF16)
    xm_ext[halo + tokens : tokens + 2 * halo, :] = jnp.zeros((halo, 128), BF16)
    xm_ext[halo : halo + tokens, :] = xm[...]
    for band in range(bands):
        at = slice(band * BAND, (band + 1) * BAND)
        dy[at, :] = (cot[at, :].astype(F32) * live_band(side * bands + band)).astype(BF16)
    tail = cot_o[...].astype(F32)
    tail = jnp.where(side == 0, tail[:W], tail[W:]) * live_band((1 - side) * bands + side * (bands - 1))
    tail = jnp.concatenate([tail, jnp.zeros((extra - W, 128), F32)], axis=0)
    dy[tokens : tokens + extra, :] = tail.astype(BF16)

    taps[...] = jnp.zeros(taps.shape, F32)
    bias[...] = jnp.zeros(bias.shape, F32)
    for part, (taps_ref, shift_ref, fc1_ref, fc2_ref) in enumerate(
        ((depth, hidden, fc1, fc2), (depth_o, hidden_o, fc1_o, fc2_o))
    ):
        lanes = slice(part * mine, part * mine + mine)
        taps[0:TAPS, lanes] = taps_ref[...]
        taps[TAPS : TAPS + 1, lanes] = shift_ref[0:1, :]
        bias[0:TAPS, lanes] = taps_ref[...] * shift_ref[0:1, :]
        bias[TAPS : TAPS + 1, lanes] = shift_ref[0:1, :] + shift_ref[1:2, :]
        fc2_t[:, lanes] = fc2_ref[...].T
        base_ref[:, lanes] = fc1_ref[...]
        base = fc1_ref[...].astype(F32)
        for k in range(TAPS):
            factor = taps_ref[k : k + 1, :] + (1.0 if k == 4 else 0.0)
            weights[k * 128 : k * 128 + 128, lanes] = (base * (factor * ROOT)).astype(BF16)
    scaled = bias[...] * ROOT
    high = scaled.astype(BF16)
    weights[TAPS * 128 : TAPS * 128 + 16, :] = high
    weights[TAPS * 128 + 16 : TAPS * 128 + 32, :] = (scaled - high.astype(F32)).astype(BF16)
    weights[TAPS * 128 + 32 : WIDE, :] = jnp.zeros((96, width), BF16)

    met(1)
    swap.start()

    def move_rows(pair, carry):
        both = xm_ext[pl.ds(pl.multiple_of(pair * halo, 16), halo), :].astype(F32)
        for i in range(2):
            row = both[W * i : W * i + W]
            moved[0, 2 * pair + i] = shift_right(row)
            moved[1, 2 * pair + i] = row
            moved[2, 2 * pair + i] = shift_left(row)
        return carry

    lax.fori_loop(1, rows // 2 + 1, move_rows, 0, unroll=2)
    swap.wait()
    xm_ext[pl.ds(halo_at, halo), :] = halo_ref[...]
    move_rows(0, 0)
    move_rows(rows // 2 + 1, 0)

    masks = mask_lanes()

    def gather_row(row, block):
        up, down = neighbour(row)
        if block == TAPS:
            return masks[0] * up + masks[1] + masks[2] * down
        a, b = divmod(block, 3)
        values = moved[b, row + a - 1]
        return values if a == 1 else values * (up if a == 0 else down)

    inner = masks[0] + masks[1] + masks[2]

    def gather_band(band, carry):
        row = 2 + 4 * band
        up, _ = neighbour(row)
        _, down = neighbour(row + 3)
        for block in range(TAPS + 1):
            if block == TAPS:
                first = masks[0] * up + masks[1] + masks[2]
                last = masks[0] + masks[1] + masks[2] * down
                parts = [first, inner, inner, last]
            else:
                a, b = divmod(block, 3)
                parts = [moved[b, row + i + a - 1] for i in range(4)]
                if a == 0:
                    parts[0] = parts[0] * up
                elif a == 2:
                    parts[3] = parts[3] * down
            both = jnp.concatenate(parts, axis=0).astype(BF16)
            wide[pl.ds(pl.multiple_of(band * BAND, 16), BAND), block * 128 : block * 128 + 128] = both
        return carry

    lax.fori_loop(0, bands, gather_band, 0)
    for block in range(TAPS + 1):
        lanes = slice(block * 128, block * 128 + 128)
        tail = jnp.concatenate([gather_row(halo_row, block), jnp.zeros((extra - W, 128), F32)], axis=0)
        wide[tokens : tokens + extra, lanes] = tail.astype(BF16)

    def fc2_part(n):
        ref, at = (fc2, n * SPAN) if n * SPAN < mine else (fc2_o, n * SPAN - mine)
        return ref[at : at + SPAN, :]

    def one_block(at, own):
        total = None
        coming = dot(wide[at, :], weights[:, 0:SPAN])
        for n in range(width // SPAN):
            lanes = slice(n * SPAN, n * SPAN + SPAN)
            spread = coming
            if (n + 1) * SPAN < width:
                coming = dot(wide[at, :], weights[:, (n + 1) * SPAN : (n + 2) * SPAN])
            grad = dot(dy[at, :], fc2_t[:, lanes])
            bell = jnp.exp2(spread * spread * -LOG2E)
            share = 1.0 + lax.erf(spread)
            du[at, lanes] = (grad * (share + spread * bell * 1.1283791670955126)).astype(BF16)
            if own:
                active = (spread * share).astype(BF16)
                act[at, lanes] = active
                part = dot(active, fc2_part(n))
                total = part if total is None else total + part
        return total

    size = 896

    def own_block(block, carry):
        at = pl.ds(pl.multiple_of(block * size, 128), size)
        for part in range(TAPS + 1):
            kept = min(128, KEPT - part * 128)
            turned = wide[at, part * 128 : part * 128 + 128].T
            wide_t[part * 128 : part * 128 + kept, at] = turned[0:kept]
        dy_t[:, at] = dy[at, :].T
        out_acc[at, :] = one_block(at, True) * ROOT
        return carry

    lax.fori_loop(0, tokens // size, own_block, 0)
    one_block(slice(tokens, tokens + extra), False)

    def fold(half):
        lanes = pl.ds(pl.multiple_of(half * SPAN, SPAN), SPAN)
        base = base_ref[:, lanes].astype(F32)
        grad = sums[4 * 128 : 5 * 128, :]
        marks = sums[TAPS * 128 : KEPT, :]
        mean = marks[TAPS : TAPS + 1]
        bias_g = mean
        rows_g = []
        factors = taps[:, lanes]
        for k in range(TAPS):
            part = sums[k * 128 : k * 128 + 128, :]
            mark = marks[k : k + 1]
            factor = factors[k : k + 1]
            grad = grad + part * factor
            bias_g = bias_g + mark * factor
            rows_g.append(jnp.sum(part * base, axis=0, keepdims=True) + mark * factors[TAPS : TAPS + 1])
        rows_g = jnp.concatenate(rows_g + [bias_g, mean, jnp.zeros((5, SPAN), F32)], axis=0)
        for i in range(SPAN // 128):
            core, row = divmod(i, STEP // 128)
            piece = slice(i * 128, i * 128 + 128)
            split_g[half, core, row * 128 : row * 128 + 128, :] = grad[:, piece] * 0.5
            split_g[half, core, 512 + 16 * row : 528 + 16 * row, :] = rows_g[:, piece] * 0.5

    def gradients(half, carry):
        lanes = pl.ds(pl.multiple_of(half * SPAN, SPAN), SPAN)
        for part in (slice(0, 592), slice(592, KEPT)):
            sums[part, :] = dot(wide_t[part, :], du[0:tokens, lanes])
        turned = dot(dy_t[...], act[:, lanes]).T * ROOT
        for core in range(2):
            split_g[half, core, 256:512, :] = turned[core * STEP : core * STEP + STEP]
        for k in range(TAPS):
            weights_t[lanes, k * 128 : k * 128 + 128] = weights[k * 128 : k * 128 + 128, lanes].T
        fold(half)
        return carry

    lax.fori_loop(0, width // SPAN, gradients, 0)

    groups = ((4, 1, 7, 0), (3, 6, 2, 5), (8,))

    def collect_row(group, base, row):
        total = [None] * 3
        for i, k in enumerate(group):
            a, b = divmod(k, 3)
            source = row + 3 - a
            part = moved[base + i, source]
            if a != 1:
                up, down = neighbour(source)
                part = part * (up if a == 0 else down)
            total[b] = part if total[b] is None else total[b] + part
        if total[0] is not None:
            total[0] = shift_left(total[0])
        if total[2] is not None:
            total[2] = shift_right(total[2])
        total = functools.reduce(jnp.add, [part for part in total if part is not None])
        at = pl.ds(pl.multiple_of(row * W, 8), W)
        if group[0] == 4:
            dxm[at, :] = total
        else:
            dxm[at, :] += total

    for number, group in enumerate(groups):
        base = 4 * (number & 1)
        for i in range(len(group)):
            moved[base + i, 1] = jnp.zeros((W, 128), F32)
            moved[base + i, rows + 2] = jnp.zeros((W, 128), F32)

        def back(at):
            parts = [weights_t[:, k * 128 : k * 128 + 128] for k in group]
            return dot(du[at, :], jnp.concatenate(parts, axis=1))

        tail = back(slice(tokens, tokens + extra))
        for i in range(len(group)):
            moved[base + i, halo_row] = tail[0:W, i * 128 : i * 128 + 128]

        def back_block(block, carry):
            result = back(pl.ds(pl.multiple_of(block * 4 * BAND, 16), 4 * BAND))
            for i in range(len(group)):
                moved[base + i, pl.ds(2 + 16 * block, 16)] = result[
                    :, i * 128 : i * 128 + 128
                ].reshape(16, W, 128)
            if number:
                for i in range(16):
                    collect_row(groups[number - 1], 4 - base, 16 * block + i)
            return carry

        lax.fori_loop(0, bands // 4, back_block, 0)

    def last_rows(row, carry):
        collect_row(groups[-1], 4 * ((len(groups) - 1) & 1), row)
        return carry

    lax.fori_loop(0, rows, last_rows, 0, unroll=4)

    mid_g[...] = jnp.zeros(mid_g.shape, F32)
    for load in loads:
        load.wait()
    place = to_slots()
    proj = proj_w[...].astype(F32)
    proj_sw = jnp.concatenate([proj[64:], proj[:64]], axis=0).T.astype(BF16)

    def one_band(band, carry):
        at = pl.ds(pl.multiple_of(band * BAND, 16), BAND)
        live = live_band(side * bands + band)
        middle = x1[at, :]
        out[at, :] = ((middle + out_acc[at, :] + shifts[3:4, :]) * live).astype(BF16)
        hat, inverse = norm_hat(middle)
        grad = dxm[at, :] * ROOT
        grad_y = dy[at, :].astype(F32)
        dx1 = grad_y + norm_back(grad * gains[1:2, :], hat, inverse)
        dx1_out[at, :] = dx1
        dz = dx1.astype(BF16)
        mid_g[8:136, :] += dot_in(heads_out[at, :], dz)
        mid_g[0:1, :] += jnp.sum(grad * hat, axis=0, keepdims=True)
        mid_g[1:2, :] += jnp.sum(grad, axis=0, keepdims=True)
        mid_g[2:3, :] += jnp.sum(dz.astype(F32), axis=0, keepdims=True)
        mid_g[3:4, :] += jnp.sum(grad_y, axis=0, keepdims=True)
        do = (dot(dz, proj_sw) * live).astype(BF16)
        do_out[band] = dot(place, do).astype(BF16)
        return carry

    lax.fori_loop(0, bands, one_band, 0, unroll=2)


def stages(levels, shared):
    rest = list(range(2, levels))
    pairs = [rest[i : i + 2] for i in range(0, len(rest), 2)]
    return [[0], ["x", 1]] + pairs if shared else [[0], [1]] + pairs + [["x"]]


def group_size(levels, rows):
    unit = 16 * 2 ** (levels - 1)
    return -(-rows // unit) * unit


def stage_shapes(levels, shared, rows):
    halves, shapes = 2, [(1, 2, rows, 128)]
    for dims in stages(levels, shared)[1:]:
        if "x" in dims:
            halves = 1
        rows >>= sum(1 for dim in dims if dim != "x")
        shapes.append((2 ** len(dims) - 1, halves, rows, 128))
    return shapes


def group_scratch(levels, shared, rows):
    buffers = [pltpu.VMEM(part, BF16) for part in stage_shapes(levels, shared, rows)]
    return [pltpu.VMEM((2, rows, 128), F32)] + buffers + buffers


def group_links(levels, shared):
    return sum(2 ** len(dims) - 1 for dims in stages(levels, shared))


def everyone(levels):
    batch, side = lax.axis_index("batch"), lax.axis_index("heads")
    peers = []
    for dims in stages(levels, True):
        for flips in range(1, 2 ** len(dims)):
            peers.append(flipped(batch, side, dims, flips))
    return peers


def flipped(batch, side, dims, flips):
    for i, dim in enumerate(dims):
        if flips >> i & 1:
            if dim == "x":
                side = 1 - side
            else:
                batch = batch + (1 - 2 * ((batch // 2**dim) % 2)) * 2**dim
    return batch, side


class Group:
    def __init__(self, levels, shared, buffers, sems, base):
        self.stages = stages(levels, shared)
        count = len(self.stages)
        self.cur, self.sends, self.recvs = buffers[0], buffers[1 : 1 + count], buffers[1 + count :]
        self.sems, self.base = sems, base
        self.batch, self.side = lax.axis_index("batch"), lax.axis_index("heads")
        self.core = self.batch % 2
        at, rows = 0, self.cur.shape[1]
        self.kept, self.given = [(at, rows)], [None]
        for dims in self.stages[1:]:
            bits = [dim for dim in dims if dim != "x"]
            starts = []
            for flips in range(2 ** len(dims)):
                batch, _ = flipped(self.batch, self.side, dims, flips)
                start = at
                for i, bit in enumerate(bits):
                    start = start + ((batch // 2**bit) % 2) * (rows >> (i + 1))
                starts.append(pl.multiple_of(start, 16))
            rows >>= len(bits)
            at = starts[0]
            self.kept.append((at, rows))
            self.given.append(starts)
        self.left = list(range(count))

    def link(self, stage, flips):
        number = self.base + sum(2 ** len(part) - 1 for part in self.stages[:stage]) + flips - 1
        peer = flipped(self.batch, self.side, self.stages[stage], flips)
        source, target = self.sends[stage].at[flips - 1], self.recvs[stage].at[flips - 1]
        return link(source, target, self.sems[0].at[number], self.sems[1].at[number], peer)

    def wait(self, stage):
        for flips in range(1, 2 ** len(self.stages[stage])):
            self.link(stage, flips).wait()

    def add(self, stage):
        at, rows = self.kept[stage]
        here, recv = pl.ds(at, rows), self.recvs[stage]
        if recv.shape[1] == 2:
            total = self.cur[:, here, :]
            for i in range(recv.shape[0]):
                total = total + recv[i].astype(F32)
            self.cur[:, here, :] = total
            return
        total = self.cur[self.side, here, :]
        for i in range(recv.shape[0]):
            total = total + recv[i, 0].astype(F32)
        self.cur[self.side, here, :] = total

    def advance(self, count=1, pieces=None):
        for number in self.left[:count]:
            self.phase(number, pieces)
        del self.left[:count]

    def phase(self, number, pieces):
        count = len(self.stages)
        if number == 0:
            for half in range(2):
                for row, value in pieces(half, 1 - self.core):
                    self.sends[0][0, half, row : row + value.shape[0], :] = value.astype(BF16)
            self.link(0, 1).start()
            for half in range(2):
                for row, value in pieces(half, self.core):
                    self.cur[half, row : row + value.shape[0], :] = value
        else:
            self.wait(number - 1)
            self.add(number - 1)
            dims = self.stages[number]
            _, rows = self.kept[number]
            for flips in range(1, 2 ** len(dims)):
                crossing = "x" in dims and flips >> dims.index("x") & 1
                here = pl.ds(self.given[number][flips], rows)
                if self.sends[number].shape[1] == 2:
                    self.sends[number][flips - 1] = self.cur[:, here, :].astype(BF16)
                else:
                    half = 1 - self.side if crossing else self.side
                    self.sends[number][flips - 1, 0] = self.cur[half, here, :].astype(BF16)
                self.link(number, flips).start()

    def finish(self):
        self.wait(len(self.stages) - 1)
        self.add(len(self.stages) - 1)
        at, rows = self.kept[-1]
        return self.cur[self.side, pl.ds(at, rows), :].astype(BF16)


class Gather:
    def __init__(self, levels, out, shared, sems, base):
        self.stages, self.out, self.shared = stages(levels, True), out, shared
        self.sems, self.base = sems, base
        self.batch, self.side = lax.axis_index("batch"), lax.axis_index("heads")
        self.core = self.batch % 2
        at, count = 0, out.shape[2]
        self.kept = [(at, count)]
        for dims in self.stages[1:]:
            for bit in dims:
                if bit != "x":
                    count //= 2
                    at = at + ((self.batch // 2**bit) % 2) * count
            self.kept.append((at, count))
        self.left = list(range(len(self.stages)))

    def links(self, stage):
        dims = self.stages[stage]
        at, count = self.kept[stage]
        number = self.base + sum(2 ** len(part) for part in self.stages[:stage])
        mine = self.out.at[self.core, self.side, pl.ds(at, count)]
        for flips in range(1, 2 ** len(dims)):
            part = mine
            if "x" in dims and flips >> dims.index("x") & 1:
                part = self.out.at[self.core, self.side, pl.ds(at, count), pl.ds(0, self.shared)]
            yield self.made(part, number, flipped(self.batch, self.side, dims, flips))
            number += 1
        if stage == 0:
            part = self.out.at[self.core, 1 - self.side, :, pl.ds(0, self.shared)]
            yield self.made(part, number, flipped(self.batch, self.side, dims, 1))

    def made(self, part, number, peer):
        return link(part, part, self.sems[0].at[number], self.sems[1].at[number], peer)

    def begin(self, pieces):
        at, _ = self.kept[-1]
        row = 0
        for piece in pieces:
            self.out[self.core, self.side, at, row : row + piece.shape[0], :] = piece
            row += piece.shape[0]
        for made in self.links(len(self.stages) - 1):
            made.start()

    def advance(self):
        stage = len(self.left) - 1
        for made in self.links(stage):
            made.wait()
        if stage:
            for made in self.links(stage - 1):
                made.start()
        del self.left[-1]


def attend_back_kernel(
    table, key_c, key_f, val_c, val_f, xn, query_t, query_o, do_ref, ot_ref, lse, output,
    dq_out, own_out, send_out, output_out,
    acc_c, acc_f, query_ref, turned_c, turned_f, keys_ref, vals_ref, kept,
):
    step = pl.program_id(0)
    each = xn.shape[0]
    bands = each * pl.num_programs(0)
    side = lax.axis_index("heads")

    @pl.when(step == 0)
    def _():
        acc_c[...] = jnp.zeros(acc_c.shape, F32)
        acc_f[...] = jnp.zeros(acc_f.shape, F32)
        query_ref[...] = full_query(query_t, query_o, side).T.astype(BF16)

    output_out[...] = output[...]
    firsts = [table[1, side * bands + each * step + i] for i in range(each)]
    for i in range(each):

        @pl.when((step == 0) | (kept[i] != firsts[i]))
        def _():
            kept[i] = firsts[i]
            keys = window(key_f, firsts[i])
            keys_ref[i] = keys
            vals_ref[i] = window(val_f, firsts[i])
            for part, (start, count) in enumerate(HALVES):
                rows = slice(start * PACKED, (start + count) * PACKED)
                turned_f[i, part, :, 0 : count * PACKED] = keys[rows].T[64:128]
            turned_c[i] = window(key_c, firsts[i]).T[0:64]

    queries, query_rows, grads_t, grads_low = [], [], [], []
    for i in range(each):
        query = dot(xn[i], query_ref[...]).astype(BF16)
        queries.append(query)
        query_rows.append(query.astype(F32).T.astype(BF16))
        grads_t.append(do_ref[i].astype(F32).T)
        grads_low.append(grads_t[i].astype(BF16))
    dq = [[None] * 4 for _ in range(each)]

    def products(unit):
        i, head, part = unit
        fine = head >= 2
        image = table[0, side * bands + each * step + i]
        start, count = HALVES[part]
        if fine:
            rows = slice(start * PACKED, (start + count) * PACKED)
            keys, vals = keys_ref[i, rows], vals_ref[i, rows]
        else:
            keys, vals = window(key_c, firsts[i]), window(val_c, firsts[i])
        swapped = (head + 2) & 3
        delta = jnp.sum(
            ot_ref[i, 32 * head : 32 * head + 32]
            * grads_t[i][32 * swapped : 32 * swapped + 32],
            axis=0,
            keepdims=True,
        )
        offset = lse[i, head : head + 1, :] * (-1.0 / EXP_SCALE)
        left = score_rows(query_rows[i], head, image, fine)
        left = with_offset(left, ONES + (0 if fine else 64), offset)
        right = with_offset(head_rows(grads_low[i], swapped), 64 if fine else 0, -delta)
        return dot(keys, left), dot(vals, right)

    held = {}

    def back(unit, score, prob_grad):
        i, head, part = unit
        fine = head >= 2
        swapped = (head + 2) & 3
        prob = jnp.exp2(score * EXP_SCALE)
        score_grad = (prob * prob_grad).astype(BF16)
        row = 32 * (head & 1)
        start, count = HALVES[part]
        turned = turned_c[i, row : row + 32]
        if fine:
            turned = turned_f[i, part, row : row + 32, 0 : count * PACKED]
        grad = dot(turned, score_grad)
        dq[i][head] = grad if part == 0 else dq[i][head] + grad
        pair = held.setdefault((i, fine, part), ([], []))
        pair[0].extend([score_grad, prob.astype(BF16)])
        pair[1].extend([head_lanes(queries[i], head), head_lanes(do_ref[i], swapped)])
        if head & 1:
            both = dot(jnp.concatenate(pair[0], axis=1), jnp.concatenate(pair[1], axis=0))
            if fine:
                at = pl.ds(firsts[i] + start, count)
                acc_f[at, 0:PACKED, :] += both.reshape(count, PACKED, 128)
            else:
                acc_c[pl.ds(firsts[i], MAX_BANDS)] += both.reshape(MAX_BANDS, COARSE, 128)

    waiting = []
    for i in range(each):
        for head, parts in ((2, 2), (3, 2), (0, 1), (1, 1)):
            for part in range(parts):
                waiting.append(((i, head, part), *products((i, head, part))))
                if len(waiting) > 3:
                    back(*waiting.pop(0))
    for unit in waiting:
        back(*unit)
    for i in range(each):
        dq_out[i] = (jnp.concatenate(dq[i], axis=0).T * SCALE).astype(BF16)

    @pl.when(step == pl.num_programs(0) - 1)
    def _():
        span = bands + 1
        lane = lax.broadcasted_iota(jnp.int32, (1, 128), 1)
        scale_c = jnp.where(lane < 64, SCALE, 1.0)
        scale_f = jnp.where(lane < 64, 1.0, SCALE)
        for dest, at, kind in (
            (own_out, side * (bands - 1), F32),
            (send_out, (1 - side) * (bands - 1), BF16),
        ):
            dest[:, 0:COARSE, :] = (acc_c[pl.ds(at, span)] * scale_c).astype(kind)
            for cell in range(4):
                part = acc_f[pl.ds(at, span), 14 * cell : 14 * cell + 16, :] * scale_f
                part = jnp.where(cell_valid(part.shape, 1), part, 0.0)
                row = COARSE + 16 * cell
                dest[:, row : row + 16, :] = part.astype(kind)


def tail_kernel(
    levels, own_in, given, split_in, mid_g, slab_in, other, meta, xn_in, hat_in, dq_in, query_t,
    query_o, dx1_in, tok_in, gains,
    red_c_in, conv_c_in, gain_c, shifts_c, kv_c, taps_c_ref,
    red_f_in, conv_f_in, gain_f, shifts_f, kv_f, taps_f_ref,
    tok_grad, joint, little,
    pack, small, small_in, small_sems, recv, grad_ref, val_ref, dxn, send_sem, recv_sem, send_sems, recv_sems, turned_c, turned_f,
    dx1, tok, hat_ref, own, split_g, slab, xn, dq, red_c, conv_c, red_f, conv_f, xt, load_sems,
    *buffers,
):
    bands = xn.shape[0]
    side = lax.axis_index("heads")
    greet(*everyone(levels))
    early_pairs = (
        (split_in, split_g), (dq_in, dq), (xn_in, xn), (own_in, own), (slab_in, slab),
        (conv_c_in, conv_c), (conv_f_in, conv_f),
    )
    loads = fetch(early_pairs, load_sems)
    met(len(everyone(levels)))
    swaps = [
        remote(given.at[:, here], recv.at[:, here], send_sem.at[i], recv_sem.at[i], across())
        for i, here in enumerate((pl.ds(0, COARSE), pl.ds(COARSE, FINE)))
    ]
    late_pairs = (
        (red_c_in, red_c), (red_f_in, red_f), (hat_in, hat_ref), (tok_in, tok), (dx1_in, dx1),
    )
    loads += fetch(late_pairs, load_sems.at[pl.ds(len(early_pairs), len(late_pairs))])
    sems = (send_sems, recv_sems)
    split_count, shared_count = (1 + 2 * len(stages(levels, shared)) for shared in (False, True))
    before = Group(levels, False, buffers[:split_count], sems, 0)
    base = group_links(levels, False)
    buffers = buffers[split_count:]
    conv = Group(levels, True, buffers[:shared_count], sems, base)
    base += group_links(levels, True)
    rest = Group(levels, True, buffers[shared_count:], sems, base)
    base += group_links(levels, True)
    early_rows, late_rows, later_rows = (group.cur.shape[1] for group in (before, conv, rest))
    gather = Gather(levels, joint, (late_rows + later_rows) // joint.shape[2], sems, base)

    def split_pieces(half, which):
        yield 0, split_g[(half + side) % 2, which]
        if early_rows > SPLIT:
            yield SPLIT, jnp.zeros((early_rows - SPLIT, 128), F32)

    def shared_pieces(first, used, rows):
        def pieces(half, which):
            at = pl.multiple_of(first + used * (2 * half + which), 16)
            yield 0, pack[pl.ds(at, used), :]
            if rows > used:
                yield used, jnp.zeros((rows - used, 128), F32)

        return pieces

    batch, order = lax.axis_index("batch"), stages(levels, True)

    def small_links(stage):
        before = sum(2 ** len(dims) - 1 for dims in order[:stage])
        for flips in range(1, 2 ** len(order[stage])):
            at = before + flips - 1
            yield at, link(
                small.at[stage], small_in.at[at], small_sems.at[0, at], small_sems.at[1, at],
                flipped(batch, side, order[stage], flips),
            )

    def small_phase(stage):
        if stage:
            total = small[stage - 1]
            for at, made in small_links(stage - 1):
                made.wait()
                total = total + small_in[at]
            if stage == len(order):
                little[...] = total
                return
            small[stage] = total
        for _, made in small_links(stage):
            made.start()

    for load in loads[:7]:
        load.wait()
    before.advance(1, split_pieces)

    start = 0
    parts = []
    for count in (conv_c.shape[0], conv_f.shape[0], 128, 128, 128, 128):
        parts.append(pack.at[start : start + count])
        start += count
    conv_c_g, conv_f_g, kv_c_g, kv_f_g, query_g, proj_g = parts
    small_c, small_f, front_g = small.at[0, 0:16], small.at[0, 16:32], small.at[0, 32:40]
    small[0, 40:48, :] = mid_g[0:8, :]
    proj_g[...] = mid_g[8:136, :]
    taps_c, taps_f = pad_taps(taps_c_ref[...], True), pad_taps(taps_f_ref[...], False)
    kv_f_sw = swap_lanes(kv_f[...])

    val_ref[0] = jnp.zeros((CELLS, 128), F32)
    val_ref[bands + 1] = jnp.zeros((CELLS, 128), F32)
    val_ref[1 : bands + 1] = slab[...]
    val_ref[pl.ds((1 - side) * (bands + 1), 1)] = other[
        pl.ds(side * (bands - 1), 1)
    ].astype(F32)
    at = pl.ds(side * bands, bands)
    above, below = meta[0, at], meta[1, at]
    grid = xn[...].reshape(bands, 16, 16, 128)
    slot_grads = dq[...].reshape(bands, 16, 16, 128)
    total = None
    for i in range(16):
        turned = grid[:, i].reshape(bands * 16, 128).T
        xt[i] = turned
        part = dot(turned, slot_grads[:, i].reshape(bands * 16, 128))
        total = part if total is None else total + part
    query_g[...] = total
    full = full_query(query_t, query_o, side).astype(BF16)
    dxn[...] = dot(dq[...].reshape(-1, 128), full).reshape(bands, SLOTS, 128)
    grad_ref[0] = jnp.zeros((CELLS, 128), F32)
    grad_ref[bands + 1] = jnp.zeros((CELLS, 128), F32)
    turned_c[...] = conv_c[...].T
    turned_f[...] = conv_f[...].T
    before.advance()
    swaps[0].wait()
    here = pl.ds(1 - side, bands + 1)
    for load in loads[7:]:
        load.wait()
    grad_ref[here, 0:COARSE] = own[:, 0:COARSE] + recv[:, 0:COARSE].astype(F32)
    lane = lax.broadcasted_iota(jnp.int32, (1, 1, 128), 2)

    def tap_sum(values, grads):
        return fold_rows(values * grads)

    def reduce_back(pair, red, conv, gain, shifts, kv, small, kv_g):
        hat, inverse = norm_hat(red[...])
        normed = hat * gain[...] + shifts[1:2, :]
        cdf, bell = gauss(normed)
        active = (normed * cdf).astype(BF16)
        kv_g[...] = dot_in(active, pair)
        small[9:10, :] = jnp.sum(pair.astype(F32), axis=0, keepdims=True)
        grad = dot_t(pair, kv) * gelu_slope(normed, cdf, bell)
        small[11:12, :] = jnp.sum(grad * hat, axis=0, keepdims=True)
        small[12:13, :] = jnp.sum(grad, axis=0, keepdims=True)
        dc = norm_back(grad * gain[...], hat, inverse).astype(BF16)
        small[13:14, :] = jnp.sum(dc.astype(F32), axis=0, keepdims=True)
        return dc

    small_c[...] = jnp.zeros(small_c.shape, F32)
    small_f[...] = jnp.zeros(small_f.shape, F32)

    vals = val_ref[:, 0:COARSE, :]
    ext = grad_ref[:, 0:COARSE, :]
    ext = jnp.where(lane < 64, ext, ext.astype(BF16).astype(F32))
    mid = ext[1:-1]
    near = (by_band(vals[:-2], above), vals[1:-1], by_band(vals[2:], below))
    for a in range(3):
        for b in range(3):
            moved = near[a] if b == 1 else roll_cells(near[a], 1 - b)
            small_c[3 * a + b : 3 * a + b + 1, :] = jnp.sum(
                tap_sum(moved, mid), axis=0, keepdims=True
            )
    small_c[10:11, :] = jnp.sum(mid.reshape(-1, 128), axis=0, keepdims=True)
    pair = mid + depthwise_coarse(ext, above, below, taps_c, flip=True)
    pair = jnp.where(cell_valid(pair.shape, 1), pair, 0.0)
    pair = pair.reshape(bands * COARSE, 128).astype(BF16)
    dc = reduce_back(pair, red_c, conv_c, gain_c, shifts_c, kv_c[...], small_c, kv_c_g)
    for i in range(16):
        part = slice(i * 128, (i + 1) * 128)
        conv_c_g[part, :] = dot(xt[i], dc)
        back = dot(dc, turned_c[:, part]).reshape(bands, 16, 128)
        dxn[:, 16 * i : 16 * i + 16, :] += back

    conv.advance(1, shared_pieces(0, CONV, late_rows))
    before.advance()
    swaps[1].wait()
    grad_ref[here, COARSE:CELLS] = own[:, COARSE:CELLS] + recv[:, COARSE:CELLS].astype(F32)
    vals = val_ref[:, COARSE:CELLS, :]
    ext = grad_ref[:, COARSE:CELLS, :]
    ext = jnp.where(lane >= 64, ext, ext.astype(BF16).astype(F32))
    rows = depthwise_fine(ext, above, below, taps_f, flip=True)
    near = fine_rows(vals, above, below)
    mids = fine_rows(ext, above, below)[1]
    for a in range(3):
        for b in range(3):
            total = jnp.zeros((8, 128), F32)
            for row in range(2):
                even, odd = near[a][row][:, 0], near[a][row][:, 1]
                grad_even, grad_odd = mids[row][:, 0], mids[row][:, 1]
                if b == 0:
                    moved = (roll_cells(odd, 1), even)
                elif b == 1:
                    moved = (even, odd)
                else:
                    moved = (odd, roll_cells(even, -1))
                total = total + tap_sum(moved[0], grad_even) + tap_sum(moved[1], grad_odd)
            small_f[3 * a + b : 3 * a + b + 1, :] = jnp.sum(total, axis=0, keepdims=True)
    small_f[10:11, :] = jnp.sum(ext[1:-1].reshape(-1, 128), axis=0, keepdims=True)
    valid = cell_valid((bands, 16, 128), 1)
    blocks = []
    for row in range(2):
        for column in range(2):
            block = jnp.where(valid, mids[row][:, column] + rows[row][column], 0.0)
            blocks.append(block.astype(BF16).reshape(bands, 1, 16, 128))
    pair = jnp.concatenate(blocks, axis=1).reshape(bands * FINE, 128)
    conv.advance()
    dc = reduce_back(pair, red_f, conv_f, gain_f, shifts_f, kv_f_sw, small_f, kv_f_g)
    for i in range(4):
        part = slice(i * 128, (i + 1) * 128)
        total = None
        for row in range(2):
            for column in range(2):
                cells = dc.reshape(bands, 4, 16, 128)[:, 2 * row + column].reshape(bands * 16, 128)
                product = dot(xt[fine_slot(i, row, column)], cells)
                total = product if total is None else total + product
        conv_f_g[part, :] = total
        back = dot(dc, turned_f[:, part]).reshape(bands, 4, 16, 128)
        for row in range(2):
            for column in range(2):
                slot = 16 * fine_slot(i, row, column)
                dxn[:, slot : slot + 16, :] += back[:, 2 * row + column]

    front_g[...] = jnp.zeros(front_g.shape, F32)
    sums = jnp.zeros((8, 128), F32)
    along = jnp.zeros((8, 128), F32)
    for band in range(bands):
        grad = dxn[band]
        sums = sums + fold_rows(grad)
        along = along + fold_rows(grad * hat_ref[band].astype(F32))
    front_g[0:1, :] = jnp.sum(along, axis=0, keepdims=True)
    front_g[1:2, :] = jnp.sum(sums, axis=0, keepdims=True)

    small_phase(0)
    rest.advance(1, shared_pieces(4 * CONV, REST, later_rows))
    conv.advance()
    before.advance()
    place = from_slots()

    def one_band(band):
        at = slice(band * BAND, (band + 1) * BAND)
        grad = dxn[band]
        high = grad.astype(BF16)
        low = (grad - high.astype(F32)).astype(BF16)
        grad = dot(place, jnp.concatenate([high, low], axis=1))
        grad = grad[:, :128] + grad[:, 128:]
        hat, inverse = norm_hat(tok[at, :].astype(F32))
        tok_grad[at, :] = dx1[at, :] + norm_back(grad * gains[0:1, :], hat, inverse)

    done, total = 0, len(rest.left) + 1 + len(gather.left)
    for number in range(1, total + 1):
        while done < bands and done * total < number * bands:
            one_band(done)
            done += 1
        if rest.left:
            rest.advance()
            conv.advance()
            before.advance()
        elif number + len(gather.left) == total:
            conv.advance(len(conv.left))
            before.advance(len(before.left))
            gather.begin([conv.finish(), rest.finish(), before.finish()])
        else:
            gather.advance()
        if number <= len(order):
            small_phase(number)


def shared_rows(start, count):
    done = 0
    while done < count:
        group = 0 if start + done < 4 * CONV else 1
        if group == 0:
            quarter, row = divmod(start + done, CONV)
            size = min(count - done, CONV - row)
        else:
            quarter, row = divmod(start + done - 4 * CONV, REST)
            size = min(count - done, REST - row)
        yield group, quarter % 2, quarter // 2, row, done, size
        done += size


def unpack_kernel(
    levels,     joint, little, tok_grad,
    tok_grad_out, gains, shifts, query, conv_c, gain_c, shifts_c, kv_c, taps_c, conv_f, gain_f, shifts_f, kv_f,
    taps_f, proj, hidden, fc1, depth, fc2,
):
    side = lax.axis_index("heads")
    half = query.shape[0]
    pieces, wide = joint.shape[2], fc2.shape[0]
    widths = [group_size(levels, part) // pieces for part in (CONV, REST, SPLIT)]
    first, second = widths[0], widths[0] + widths[1]
    spans = (slice(0, first), slice(first, second), slice(second, second + widths[2]))

    def quarter_rows(group, core, h):
        return joint[core, h, :, spans[group], :].reshape(-1, 128)

    tok_grad_out[...] = tok_grad[...]

    def rows_of(start, count):
        pieces = [
            quarter_rows(group, core, h)[at : at + size].astype(F32)
            for group, core, h, at, _, size in shared_rows(start, count)
        ]
        return pieces[0] if len(pieces) == 1 else jnp.concatenate(pieces, axis=0)

    start = 0
    for ref in (conv_c, conv_f, kv_c):
        count = ref.shape[0]
        for group, core, h, at, offset, size in shared_rows(start, count):
            ref[offset : offset + size, :] = quarter_rows(group, core, h)[at : at + size].astype(F32)
        start += count
    kv_f[...] = swap_lanes(rows_of(start, 128))
    both = rows_of(start + 128, 128)
    query[...] = jnp.where(side == 0, both[:, :half], both[:, half:]).T
    proj[...] = rows_of(start + 256, 128)
    small = little[...]
    coarse, fine, front, mid = small[0:16], small[16:32], small[32:40], small[40:48]
    taps_c[...] = coarse[0:9, half:]
    taps_f[...] = fine[0:9, :half]
    gain_c[...] = coarse[11:12]
    gain_f[...] = fine[11:12]
    shifts_c[0:1, :] = coarse[13:14]
    shifts_c[1:2, :] = coarse[12:13]
    shifts_c[2:3, :] = jnp.concatenate([coarse[9:10, half:], coarse[10:11, half:]], axis=1)
    shifts_f[0:1, :] = fine[13:14]
    shifts_f[1:2, :] = fine[12:13]
    shifts_f[2:3, :] = jnp.concatenate([fine[9:10, :half], fine[10:11, :half]], axis=1)
    gains[0:1, :] = front[0:1]
    gains[1:2, :] = mid[0:1]
    shifts[0:1, :] = front[1:2]
    shifts[1:2, :] = mid[2:3]
    shifts[2:3, :] = mid[1:2]
    shifts[3:4, :] = mid[3:4]
    for core in range(2):
        split = quarter_rows(2, core, side)
        for i in range(2):
            lanes = slice(core * STEP + i * 128, core * STEP + i * 128 + 128)
            fc1[:, lanes] = split[i * 128 : i * 128 + 128].astype(F32)
            block = split[512 + 16 * i : 528 + 16 * i].astype(F32)
            depth[:, lanes] = block[0:9]
            hidden[:, lanes] = block[9:11]
        fc2[core * STEP : core * STEP + STEP, :] = split[256:512].astype(F32)


SMEM = pl.BlockSpec(memory_space=pltpu.SMEM)
VMEM = pl.BlockSpec(memory_space=pltpu.VMEM)
HBM = pl.BlockSpec(memory_space=pl.ANY)


def shape(dims, kind=F32):
    return jax.ShapeDtypeStruct(dims, kind)


def params(limit=56):
    return pltpu.CompilerParams(vmem_limit_bytes=limit * MIB)


def sending(number, limit=56):
    return pltpu.CompilerParams(
        vmem_limit_bytes=limit * MIB, collective_id=number, has_side_effects=True
    )


def per_device(
    size, tokens, image_bands, cotangent, front_gains, front_shifts, query_w, coarse_conv,
    coarse_gain, coarse_shifts, coarse_kv, coarse_taps, fine_conv, fine_gain, fine_shifts, fine_kv,
    fine_taps, proj_w, hidden_shifts, fc1_w, depth_taps, fc2_w,
):
    count = tokens.shape[0]
    rows = count // W
    bands = count // BAND
    total = 2 * bands
    halo = 2 * W
    half = coarse_kv.shape[1] // 2
    mine = fc1_w.shape[1]
    hidden = 2 * mine
    gain_c, gain_f = coarse_gain[None], fine_gain[None]
    semaphores = pltpu.SemaphoreType.DMA
    levels = size.bit_length() - 1
    query_t = query_w.T

    (
        table, meta, xn, hat, red_c, red_f, slab, other, query_o,
    ) = pl.pallas_call(
        front_kernel,
        out_shape=(
            shape((3, 32), jnp.int32),
            shape((3, total, 8, 128)),
            shape((bands, SLOTS, 128), BF16),
            shape((bands, SLOTS, 128), BF16),
            shape((bands * COARSE, 128)),
            shape((bands * FINE, 128)),
            shape((bands, CELLS, 128)),
            shape((bands, CELLS, 128), BF16),
            shape(query_t.shape, BF16),
        ),
        in_specs=[SMEM] + [VMEM] * 12,
        out_specs=[SMEM] + [VMEM] * 8,
        scratch_shapes=[pltpu.VMEM((bands, CELLS, 128), BF16), semaphores((8,)), semaphores((8,))],
        compiler_params=sending(1),
        name="front",
    )(
        image_bands, tokens, front_gains, front_shifts, coarse_conv, gain_c, coarse_shifts,
        coarse_kv, fine_conv, gain_f, fine_shifts, fine_kv,
        query_t,
    )

    each = 4 if bands % 4 == 0 else 2
    some_bands = pl.BlockSpec((each * BAND, 128), lambda i: (i, 0))
    some_slots = pl.BlockSpec((each, SLOTS, 128), lambda i: (i, 0, 0))
    two_slots = pl.BlockSpec((2, SLOTS, 128), lambda i: (i, 0, 0))
    (
        x1, xm, heads_out, out_t, lse, key_c, key_f, val_c, val_f, fc1_o, fc2_o, depth_o, hidden_o,
        cot_o,
    ) = pl.pallas_call(
        attend_kernel,
        grid=(bands // each,),
        out_shape=(
            shape((count, 128)),
            shape((count, 128), BF16),
            shape((count, 128), BF16),
            shape((bands, 128, SLOTS)),
            shape((bands, 8, SLOTS)),
            shape((total, COARSE, 128), BF16),
            shape((total, PACKED, 128)),
            shape((total, COARSE, 128), BF16),
            shape((total, PACKED, 128)),
            shape(fc1_w.shape, BF16),
            shape(fc2_w.shape, BF16),
            shape(depth_taps.shape),
            shape(hidden_shifts.shape),
            shape((halo, 128), BF16),
        ),
        in_specs=[SMEM] + [VMEM] * 7 + [some_slots, some_bands] + [VMEM] * 5 + [HBM] * 5,
        out_specs=[
            some_bands,
            some_bands,
            some_bands,
            pl.BlockSpec((each, 128, SLOTS), lambda i: (i, 0, 0)),
            pl.BlockSpec((each, 8, SLOTS), lambda i: (i, 0, 0)),
        ]
        + [VMEM] * 4
        + [HBM] * 5,
        scratch_shapes=[
            pltpu.VMEM((total + 2, CELLS, 128), F32),
            pltpu.VMEM((128, 128), BF16),
            pltpu.VMEM((BAND, SLOTS), BF16),
            semaphores((5,)),
            semaphores((5,)),
        ],
        compiler_params=sending(4),
        name="attend",
    )(
        table, slab, other, meta, coarse_taps, fine_taps, coarse_shifts, fine_shifts, xn, tokens,
        query_t, query_o, proj_w, front_gains, front_shifts, fc1_w, fc2_w, depth_taps,
        hidden_shifts, cotangent,
    )

    extra = 64
    output, dx1, out_grad, split_g, mid_g = pl.pallas_call(
        hidden_kernel,
        out_shape=(
            shape((count, 128), BF16),
            shape((count, 128)),
            shape((bands, SLOTS, 128), BF16),
            shape((2, 2, SPLIT, 128)),
            shape((136, 128)),
        ),
        in_specs=[SMEM, HBM] + [VMEM] * 3 + [HBM] + [VMEM] * 11,
        out_specs=[VMEM] * 5,
        scratch_shapes=[
            pltpu.VMEM((count + 2 * halo, 128), BF16),
            pltpu.VMEM((halo, 128), BF16),
            pltpu.VMEM((8, rows + 4, W, 128), F32),
            pltpu.VMEM((count + extra, WIDE), BF16),
            pltpu.VMEM((KEPT, count), BF16),
            pltpu.VMEM((WIDE, hidden), BF16),
            pltpu.VMEM((hidden, TAPS * 128), BF16),
            pltpu.VMEM((16, hidden), F32),
            pltpu.VMEM((16, hidden), F32),
            pltpu.VMEM((128, hidden), BF16),
            pltpu.VMEM((128, hidden), BF16),
            pltpu.VMEM((count + extra, 128), BF16),
            pltpu.VMEM((128, count), BF16),
            pltpu.VMEM((count, hidden), BF16),
            pltpu.VMEM((count + extra, hidden), BF16),
            pltpu.VMEM((KEPT, SPAN), F32),
            pltpu.VMEM((count, 128), F32),
            pltpu.VMEM((count, 128), F32),
            pltpu.VMEM((count, 128), F32),
            pltpu.VMEM((count, 128), BF16),
            semaphores(()),
            semaphores(()),
            semaphores((2,)),
        ],
        compiler_params=sending(2, 63),
        name="hidden",
    )(
        table, x1, xm, cotangent, cot_o, heads_out, fc1_w, fc1_o, fc2_w, fc2_o, depth_taps, depth_o,
        hidden_shifts, hidden_o, front_gains, front_shifts, proj_w,
    )

    dq, grad_own, grad_send, output = pl.pallas_call(
        attend_back_kernel,
        grid=(bands // 2,),
        out_shape=(
            shape((bands, SLOTS, 128), BF16),
            shape((bands + 1, CELLS, 128)),
            shape((bands + 1, CELLS, 128), BF16),
            shape((count, 128), BF16),
        ),
        in_specs=[SMEM]
        + [VMEM] * 4
        + [
            two_slots,
            VMEM,
            VMEM,
            two_slots,
            pl.BlockSpec((2, 128, SLOTS), lambda i: (i, 0, 0)),
            pl.BlockSpec((2, 8, SLOTS), lambda i: (i, 0, 0)),
            pl.BlockSpec((2 * BAND, 128), lambda i: (i, 0)),
        ],
        out_specs=[two_slots, VMEM, VMEM, pl.BlockSpec((2 * BAND, 128), lambda i: (i, 0))],
        scratch_shapes=[
            pltpu.VMEM((total, COARSE, 128), F32),
            pltpu.VMEM((total, FINE, 128), F32),
            pltpu.VMEM((128, 128), BF16),
            pltpu.VMEM((2, 64, MAX_BANDS * COARSE), BF16),
            pltpu.VMEM((2, 2, 64, HALVES[0][1] * PACKED), BF16),
            pltpu.VMEM((2, MAX_BANDS * PACKED, 128), BF16),
            pltpu.VMEM((2, MAX_BANDS * PACKED, 128), BF16),
            pltpu.SMEM((2,), jnp.int32),
        ],
        compiler_params=params(),
        name="attend_back",
    )(table, key_c, key_f, val_c, val_f, xn, query_t, query_o, out_grad, out_t, lse, output)

    peers = sum(2 ** len(dims) - 1 for dims in stages(levels, True))
    links = group_links(levels, False) + 3 * group_links(levels, True) + len(stages(levels, True)) + 1
    early_rows, late_rows, later_rows = (group_size(levels, part) for part in (SPLIT, CONV, REST))
    pieces = 2 ** (levels - 1)
    joint_rows = (early_rows + late_rows + later_rows) // pieces
    tokens_grad, joint, little = pl.pallas_call(
        functools.partial(tail_kernel, levels),
        out_shape=(
            shape((count, 128)),
            shape((2, 2, pieces, joint_rows, 128), BF16),
            shape((SMALL, 128)),
        ),
        in_specs=[HBM] * 3 + [VMEM, HBM] + [VMEM] * 2 + [HBM] * 3 + [VMEM] * 2 + [HBM] * 2
        + [VMEM] + ([HBM] * 2 + [VMEM] * 4) * 2,
        out_specs=[VMEM] * 3,
        scratch_shapes=[
            pltpu.VMEM((4 * QUARTER, 128), F32),
            pltpu.VMEM((len(stages(levels, True)), SMALL, 128), F32),
            pltpu.VMEM((peers, SMALL, 128), F32),
            semaphores((2, peers)),
            pltpu.VMEM((bands + 1, CELLS, 128), BF16),
            pltpu.VMEM((bands + 2, CELLS, 128), F32),
            pltpu.VMEM((bands + 2, CELLS, 128), F32),
            pltpu.VMEM((bands, SLOTS, 128), F32),
            semaphores((2,)),
            semaphores((2,)),
            semaphores((links,)),
            semaphores((links,)),
            pltpu.VMEM((128, coarse_conv.shape[0]), BF16),
            pltpu.VMEM((128, fine_conv.shape[0]), BF16),
            pltpu.VMEM((count, 128), F32),
            pltpu.VMEM((count, 128), BF16),
            pltpu.VMEM((bands, SLOTS, 128), BF16),
            pltpu.VMEM(grad_own.shape, F32),
            pltpu.VMEM(split_g.shape, F32),
            pltpu.VMEM(slab.shape, F32),
            pltpu.VMEM(xn.shape, BF16),
            pltpu.VMEM(dq.shape, BF16),
            pltpu.VMEM(red_c.shape, F32),
            pltpu.VMEM(coarse_conv.shape, BF16),
            pltpu.VMEM(red_f.shape, F32),
            pltpu.VMEM(fine_conv.shape, BF16),
            pltpu.VMEM((16, 128, bands * 16), BF16),
            semaphores((12,)),
        ]
        + group_scratch(levels, False, early_rows)
        + group_scratch(levels, True, late_rows)
        + group_scratch(levels, True, later_rows),
        compiler_params=sending(0),
        name="tail",
    )(
        grad_own, grad_send, split_g, mid_g, slab, other, meta, xn, hat, dq, query_t, query_o, dx1,
        tokens, front_gains,
        red_c, coarse_conv, gain_c, coarse_shifts, coarse_kv, coarse_taps,
        red_f, fine_conv, gain_f, fine_shifts, fine_kv, fine_taps,
    )
    grads = pl.pallas_call(
        functools.partial(unpack_kernel, levels),
        out_shape=(
            shape((count, 128)),
            shape((2, 128)),
            shape((4, 128)),
            shape((half, 128)),
            shape(coarse_conv.shape),
            shape((1, 128)),
            shape((3, 128)),
            shape((128, 128)),
            shape((9, half)),
            shape(fine_conv.shape),
            shape((1, 128)),
            shape((3, 128)),
            shape((128, 128)),
            shape((9, half)),
            shape((128, 128)),
            shape((2, mine)),
            shape((128, mine)),
            shape((9, mine)),
            shape((mine, 128)),
        ),
        in_specs=[VMEM] * 3,
        out_specs=[VMEM] * 19,
        compiler_params=params(),
        name="unpack",
    )(joint, little, tokens_grad)
    grads = [output] + list(grads)
    grads[4] = grads[4].T
    for at in (6, 11):
        grads[at] = grads[at].reshape(128)
    return tuple(grads)


def solution(mesh):
    tokens = P(("batch", "heads"), None)
    columns = P(None, "heads")
    return jax.shard_map(
        functools.partial(per_device, mesh.shape["batch"]),
        mesh=mesh,
        in_specs=(tokens, P("batch", None), tokens, P(), P(), columns)
        + (P(),) * 11
        + (columns, columns, columns, P("heads", None)),
        out_specs=(tokens, tokens, P(), P(), columns)
        + (P(),) * 11
        + (columns, columns, columns, P("heads", None)),
        check_vma=False,
    )
```

time: 1060 us -> 142 us (0.13)
  waiting for transfers between devices: 364 us -> 0 us
  other arithmetic: 251 us -> 0 us
  blocking collectives: 212 us -> 0 us
  Pallas kernels: 0 us -> 141 us
  local copies, waits for them, and re-layouts: 102 us -> 0 us
  matrix products: 87.1 us -> 0 us
  loops' own time: 17.2 us -> 0 us
  between operations: 15.4 us -> 0.71 us
    psum x4 -> x0, waiting for transfers between devices: 258 us -> none  [the longest x2 135 us: norm_sum(): lax.psum(partial_grad.astype(jnp.bfloat16), 'heads').astype(jnp.float32)]
    psum x2 -> x0, blocking collectives: 178 us -> none  [the longest x1 116 us: per_device(): lax.psum((front_gains_grad, front_shifts_grad, proj_grad, coarse_conv_gra...]
    pallas_call x0 -> x6, Pallas kernels: none -> 141 us  [the longest x1 45.3 us: per_device(): pl.pallas_call(hidden_kernel, out_shape=(shape((count, 128), BF16), shape...]
    add x7 -> x0, other arithmetic: 107 us -> none  [the longest x4 101 us: depthwise_ext(): result + padded[above:above + grid_rows, across:across + grid_cols] * tap...]
    reduce_sum x24 -> x0, other arithmetic: 92.4 us -> none  [the longest x4 62.8 us: tap_grads_ext(): collected.append(jnp.sum(shifted * grad_grid * same_image, axis=(0, 1)))]
    dot_general x62 -> x0, matrix products: 87.1 us -> none  [the longest x12 19.8 us: one_block(): jnp.einsum('lfq,tfq->flt', query_block_rows, key_head_rows, preferred_ele...]
    all_gather x3 -> x0, waiting for transfers between devices: 71.6 us -> none  [the longest x1 25 us: per_device(): grad_full = lax.all_gather(grad_own_b, 'heads', axis=0, tiled=True)]
    convert_element_type x17 -> x0, other arithmetic: 35.3 us -> none  [the longest x1 27.8 us: per_device(): activated = gelu_value(spread).astype(jnp.bfloat16)]
  transfers between devices with their start and end apart: 9 -> 0, of which waited for: 8 -> 0; matrix products, arithmetic and copies ran while one was open for 8% -> 0% of each run, Pallas kernels for 0% -> 0%
where the time goes in v1:
time: 142 us
  Pallas kernels  141 us (99%)
    pallas_call x1, Pallas kernels, per_device(): pl.pallas_call(hidden_kernel, out_shape=(shape((count, 128), BF16), shape...  45.3 us
    pallas_call x1, Pallas kernels, per_device(): pl.pallas_call(functools.partial(tail_kernel, levels), out_shape=(shape((...  40.6 us
    pallas_call x1, Pallas kernels, per_device(): pl.pallas_call(attend_back_kernel, grid=(bands // 2,), out_shape=(shape((...  21.1 us
    pallas_call x1, Pallas kernels, per_device(): pl.pallas_call(attend_kernel, grid=(bands // each,), out_shape=(shape((co...  15.8 us
    pallas_call x1, Pallas kernels, per_device(): pl.pallas_call(front_kernel, out_shape=(shape((3, 32), jnp.int32), shape(...  14.5 us
    pallas_call x1, Pallas kernels, per_device(): pl.pallas_call(functools.partial(unpack_kernel, levels), out_shape=(shape...  3.68 us

profile of v1, /device:TPU:0, one launch (start us, length us, event | category | flops | bytes accessed | tf_op | source)
XLA Modules:
  0.0 141.8 jit_solution(3572327716169940214)
XLA Ops:
  0.7 14.5 %front.1 = (s32[3,32]{1,0:T(4,128)}, f32[3,24,8,128]{3,2,1,0:T(8,128)}, bf16[12,256,128]{2,1,0:T(8,128)(2,1)}, bf16[12,256,128]{2,1,0:T(8,128)(2,1)}, f32[192,12...) custom-call(s32[1,24]{1,0:T(1,128)} %heights.1, ...), custom_call_target="tpu_custom_call" | custom-call | tf_op jit(solution)/shard_map/front/pallas_call | solution.py:1505
  15.2 15.8 %attend.1 = (f32[2688,128]{1,0:T(8,128)}, bf16[2688,128]{1,0:T(8,128)(2,1)}, bf16[2688,128]{1,0:T(8,128)(2,1)}, f32[12,128,256]{2,1,0:T(8,128)}, f32[12,8,256]{2...) custom-call(s32[3,32]{1,0:T(4,128)} %get-tuple-element.74.table, ...), custom_call_target="tpu_custom_call" | custom-call | tf_op jit(solution)/shard_map/attend/pallas_call | solution.py:1536
  31.0 45.3 %hidden.4 = (bf16[2688,128]{1,0:T(8,128)(2,1)}, f32[2688,128]{1,0:T(8,128)}, bf16[12,256,128]{2,1,0:T(8,128)(2,1)}, f32[2,2,544,128]{3,2,1,0:T(8,128)}, f32[136,128]{1,0:T(8,128)}) custom-call(s32[3,32]{1,0:T(4,128)} %get-tuple-element.74.table, f32[2688,128]{1,0:T(8,128)} %get-tuple-element.84.x1_in, bf16[2688,128]{1,0:T(8,128)(2,1)} %get-tuple-element.85.xm, ...), custom_call_target="tpu_custom_call" | custom-call | tf_op jit(solution)/shard_map/hidden/pallas_call | solution.py:1581
  76.3 21.1 %attend_back.1 = (bf16[12,256,128]{2,1,0:T(8,128)(2,1)}, f32[13,80,128]{2,1,0:T(8,128)}, bf16[13,80,128]{2,1,0:T(8,128)(2,1)}, bf16[2688,128]{1,0:T(8,128)(2,1)}) custom-call(s32[3,32]{1,0:T(4,128)} %get-tuple-element.74.table, bf16[24,16,128]{2,1,0:T(8,128)(2,1)} %get-tuple-element.80.key_c, f32[24,56,128]{2,1,0:T(8,128)} %get-tuple-element.81.key_f, ...), custom_call_target="tpu_custom_call" | custom-call | tf_op jit(solution)/shard_map/attend_back/pallas_call | solution.py:1624
  97.4 40.6 %tail.1 = (f32[2688,128]{1,0:T(8,128)}, bf16[2,2,8,176,128]{4,3,2,1,0:T(8,128)(2,1)}, f32[48,128]{1,0:T(8,128)}) custom-call(f32[13,80,128]{2,1,0:T(8,128)} %get-tuple-element.97.own_in, bf16[13,80,128]{2,1,0:T(8,128)(2,1)} %get-tuple-element.98.given, f32[2,2,544,128]{3,2,1,0:T(8,128)} %get-tuple-element.99.split_in, f32[136,128]{1,0:T(8,128)} %get-tuple-element.100.mid_g, ...), custom_call_target="tpu_custom_call" | custom-call | tf_op jit(solution)/shard_map/tail/pallas_call | solution.py:1664
  138.1 3.7 %unpack.1 = (f32[2688,128]{1,0:T(8,128)}, f32[2,128]{1,0:T(2,128)}, f32[4,128]{1,0:T(4,128)}, f32[64,128]{1,0:T(8,128)}, f32[2048,128]{1,0:T(8,128)}, /*index=5*...) custom-call(bf16[2,2,8,176,128]{4,3,2,1,0:T(8,128)(2,1)} %get-tuple-, ...), custom_call_target="tpu_custom_call" | custom-call | tf_op jit(solution)/shard_map/unpack/pallas_call | solution.py:1715

commit v2 on v1

--- a/solution.py
+++ b/solution.py
@@ -231,7 +231,7 @@
 def front_kernel(
     heights, tok, gains, shifts, conv_c, gain_c, shifts_c, kv_c, conv_f, gain_f, shifts_f, kv_f,
     query_t,
-    table, meta, xn_out, hat_out, red_c, red_f, slab, other, query_o,
+    table, meta, xn_out, hat_out, inv_out, red_c, red_f, slab, other, query_o,
     send, send_sems, recv_sems,
 ):
     bands = xn_out.shape[0]
@@ -245,14 +245,16 @@
 
     place = to_slots()
 
-    def one_band(band, carry):
-        values = tok[pl.ds(pl.multiple_of(band * BAND, 16), BAND), :].astype(F32)
-        hat, _ = norm_hat(values)
+    def norm_bands(first, count):
+        rows = slice(first * BAND, (first + count) * BAND)
+        hat, inverse = norm_hat(tok[rows, :].astype(F32))
+        inv_out[rows, :] = jnp.broadcast_to(inverse, hat.shape)
         normed = (hat * gains[0:1, :] + shifts[0:1, :]).astype(BF16)
-        both = dot(place, jnp.concatenate([normed, hat.astype(BF16)], axis=1)).astype(BF16)
-        xn_out[band] = both[:, :128]
-        hat_out[band] = both[:, 128:]
-        return carry
+        sides = jnp.concatenate([normed, hat.astype(BF16)], axis=1)
+        for band in range(count):
+            both = dot(place, sides[band * BAND : (band + 1) * BAND]).astype(BF16)
+            xn_out[first + band] = both[:, :128]
+            hat_out[first + band] = both[:, 128:]
 
     def reduce(patches, conv, gain, shift, kv, out, at):
         red = dot(patches, conv) + shift[0:1, :]
@@ -265,7 +267,7 @@
     kv_f_sw = swap_lanes(kv_f[...])
     part = bands // 2
     for first in (0, part):
-        lax.fori_loop(first, first + part, one_band, 0, unroll=2)
+        norm_bands(first, part)
         grid = xn_out[first : first + part].reshape(part, 16, 16, 128)
         patches = jnp.concatenate([fine_patch(grid, i) for i in range(4)], axis=1)
         pair = reduce(patches, conv_f[...], gain_f, shifts_f, kv_f_sw, red_f, first * FINE)
@@ -494,17 +496,18 @@
     for unit, scores in waiting:
         mix(unit, scores)
     place = place_ref[...]
+    joined = []
     for i in range(each):
         live = jnp.where(images[i] >= 0, 1.0, 0.0)
         out_t = jnp.concatenate(outs[i], axis=0) * live
         ot_out[i] = out_t
-        heads_out = dot(place, out_t.T.astype(BF16)).astype(BF16)
-        at = slice(i * BAND, (i + 1) * BAND)
-        o_out[at, :] = heads_out
-        middle = tok[at, :].astype(F32) + dot(heads_out, proj_w[...]) + shifts[1:2, :]
-        x1_out[at, :] = middle
-        hat, _ = norm_hat(middle)
-        xm_out[at, :] = (hat * gains[1:2, :] + shifts[2:3, :]).astype(BF16)
+        joined.append(dot(place, out_t.T.astype(BF16)).astype(BF16))
+    heads_out = jnp.concatenate(joined, axis=0)
+    o_out[...] = heads_out
+    middle = tok[...].astype(F32) + dot(heads_out, proj_w[...]) + shifts[1:2, :]
+    x1_out[...] = middle
+    hat, _ = norm_hat(middle)
+    xm_out[...] = (hat * gains[1:2, :] + shifts[2:3, :]).astype(BF16)
 
     @pl.when(step == pl.num_programs(0) - 1)
     def _():
@@ -796,11 +799,13 @@
     proj = proj_w[...].astype(F32)
     proj_sw = jnp.concatenate([proj[64:], proj[:64]], axis=0).T.astype(BF16)
 
-    def one_band(band, carry):
-        at = pl.ds(pl.multiple_of(band * BAND, 16), BAND)
-        live = live_band(side * bands + band)
+    def fold_up(values):
+        return jnp.sum(jnp.sum(values.reshape(-1, 64, 128), axis=0).reshape(8, 8, 128), axis=0)
+
+    def two_bands(block, carry):
+        at = pl.ds(pl.multiple_of(block * 2 * BAND, 16), 2 * BAND)
         middle = x1[at, :]
-        out[at, :] = ((middle + out_acc[at, :] + shifts[3:4, :]) * live).astype(BF16)
+        result = middle + out_acc[at, :] + shifts[3:4, :]
         hat, inverse = norm_hat(middle)
         grad = dxm[at, :] * ROOT
         grad_y = dy[at, :].astype(F32)
@@ -808,15 +813,21 @@
         dx1_out[at, :] = dx1
         dz = dx1.astype(BF16)
         mid_g[8:136, :] += dot_in(heads_out[at, :], dz)
-        mid_g[0:1, :] += jnp.sum(grad * hat, axis=0, keepdims=True)
-        mid_g[1:2, :] += jnp.sum(grad, axis=0, keepdims=True)
-        mid_g[2:3, :] += jnp.sum(dz.astype(F32), axis=0, keepdims=True)
-        mid_g[3:4, :] += jnp.sum(grad_y, axis=0, keepdims=True)
-        do = (dot(dz, proj_sw) * live).astype(BF16)
-        do_out[band] = dot(place, do).astype(BF16)
-        return carry
-
-    lax.fori_loop(0, bands, one_band, 0, unroll=2)
+        do = dot(dz, proj_sw)
+        for i in range(2):
+            band = 2 * block + i
+            live = live_band(side * bands + band)
+            part = slice(i * BAND, (i + 1) * BAND)
+            here = pl.ds(pl.multiple_of(band * BAND, 16), BAND)
+            out[here, :] = (result[part] * live).astype(BF16)
+            do_out[band] = dot(place, (do[part] * live).astype(BF16)).astype(BF16)
+        terms = (grad * hat, grad, dz.astype(F32), grad_y)
+        return tuple(total + fold_up(term) for total, term in zip(carry, terms))
+
+    zero = jnp.zeros((8, 128), F32)
+    totals = lax.fori_loop(0, bands // 2, two_bands, (zero,) * 4)
+    for i in range(4):
+        mid_g[i : i + 1, :] = jnp.sum(totals[i], axis=0, keepdims=True)
 
 
 def stages(levels, shared):
@@ -1128,12 +1139,12 @@
 
 def tail_kernel(
     levels, own_in, given, split_in, mid_g, slab_in, other, meta, xn_in, hat_in, dq_in, query_t,
-    query_o, dx1_in, tok_in, gains,
+    query_o, dx1_in, inv_in, gains,
     red_c_in, conv_c_in, gain_c, shifts_c, kv_c, taps_c_ref,
     red_f_in, conv_f_in, gain_f, shifts_f, kv_f, taps_f_ref,
     tok_grad, joint, little,
     pack, small, small_in, small_sems, recv, grad_ref, val_ref, dxn, send_sem, recv_sem, send_sems, recv_sems, turned_c, turned_f,
-    dx1, tok, hat_ref, own, split_g, slab, xn, dq, red_c, conv_c, red_f, conv_f, xt, load_sems,
+    dx1, inv, hat_ref, own, split_g, slab, xn, dq, red_c, conv_c, red_f, conv_f, xt, load_sems,
     *buffers,
 ):
     bands = xn.shape[0]
@@ -1150,7 +1161,7 @@
         for i, here in enumerate((pl.ds(0, COARSE), pl.ds(COARSE, FINE)))
     ]
     late_pairs = (
-        (red_c_in, red_c), (red_f_in, red_f), (hat_in, hat_ref), (tok_in, tok), (dx1_in, dx1),
+        (red_c_in, red_c), (red_f_in, red_f), (hat_in, hat_ref), (inv_in, inv), (dx1_in, dx1),
     )
     loads += fetch(late_pairs, load_sems.at[pl.ds(len(early_pairs), len(late_pairs))])
     sems = (send_sems, recv_sems)
@@ -1359,13 +1370,8 @@
 
     def one_band(band):
         at = slice(band * BAND, (band + 1) * BAND)
-        grad = dxn[band]
-        high = grad.astype(BF16)
-        low = (grad - high.astype(F32)).astype(BF16)
-        grad = dot(place, jnp.concatenate([high, low], axis=1))
-        grad = grad[:, :128] + grad[:, 128:]
-        hat, inverse = norm_hat(tok[at, :].astype(F32))
-        tok_grad[at, :] = dx1[at, :] + norm_back(grad * gains[0:1, :], hat, inverse)
+        back = norm_back(dxn[band] * gains[0:1, :], hat_ref[band].astype(F32), 1.0)
+        tok_grad[at, :] = dx1[at, :] + dot(place, back.astype(BF16)) * inv[at, :]
 
     done, total = 0, len(rest.left) + 1 + len(gather.left)
     for number in range(1, total + 1):
@@ -1501,7 +1507,7 @@
     query_t = query_w.T
 
     (
-        table, meta, xn, hat, red_c, red_f, slab, other, query_o,
+        table, meta, xn, hat, inverse, red_c, red_f, slab, other, query_o,
     ) = pl.pallas_call(
         front_kernel,
         out_shape=(
@@ -1509,6 +1515,7 @@
             shape((3, total, 8, 128)),
             shape((bands, SLOTS, 128), BF16),
             shape((bands, SLOTS, 128), BF16),
+            shape((count, 128)),
             shape((bands * COARSE, 128)),
             shape((bands * FINE, 128)),
             shape((bands, CELLS, 128)),
@@ -1516,7 +1523,7 @@
             shape(query_t.shape, BF16),
         ),
         in_specs=[SMEM] + [VMEM] * 12,
-        out_specs=[SMEM] + [VMEM] * 8,
+        out_specs=[SMEM] + [VMEM] * 9,
         scratch_shapes=[pltpu.VMEM((bands, CELLS, 128), BF16), semaphores((8,)), semaphores((8,))],
         compiler_params=sending(1),
         name="front",
@@ -1687,7 +1694,7 @@
             pltpu.VMEM((128, coarse_conv.shape[0]), BF16),
             pltpu.VMEM((128, fine_conv.shape[0]), BF16),
             pltpu.VMEM((count, 128), F32),
-            pltpu.VMEM((count, 128), BF16),
+            pltpu.VMEM((count, 128), F32),
             pltpu.VMEM((bands, SLOTS, 128), BF16),
             pltpu.VMEM(grad_own.shape, F32),
             pltpu.VMEM(split_g.shape, F32),
@@ -1708,7 +1715,7 @@
         name="tail",
     )(
         grad_own, grad_send, split_g, mid_g, slab, other, meta, xn, hat, dq, query_t, query_o, dx1,
-        tokens, front_gains,
+        inverse, front_gains,
         red_c, coarse_conv, gain_c, coarse_shifts, coarse_kv, coarse_taps,
         red_f, fine_conv, gain_f, fine_shifts, fine_kv, fine_taps,
     )

time: 142 us -> 140 us (0.986)
  Pallas kernels: 141 us -> 139 us
where the time goes in v2:
time: 140 us
  Pallas kernels  139 us (99%)
    pallas_call x1, Pallas kernels, per_device(): pl.pallas_call(hidden_kernel, out_shape=(shape((count, 128), BF16), shape...  44.6 us
    pallas_call x1, Pallas kernels, per_device(): pl.pallas_call(functools.partial(tail_kernel, levels), out_shape=(shape((...  40.7 us
    pallas_call x1, Pallas kernels, per_device(): pl.pallas_call(attend_back_kernel, grid=(bands // 2,), out_shape=(shape((...  20.8 us
    pallas_call x1, Pallas kernels, per_device(): pl.pallas_call(attend_kernel, grid=(bands // each,), out_shape=(shape((co...  15.3 us
    pallas_call x1, Pallas kernels, per_device(): pl.pallas_call(front_kernel, out_shape=(shape((3, 32), jnp.int32), shape(...  14.3 us
    pallas_call x1, Pallas kernels, per_device(): pl.pallas_call(functools.partial(unpack_kernel, levels), out_shape=(shape...  3.68 us

profile of v2, /device:TPU:0, one launch (start us, length us, event | category | flops | bytes accessed | tf_op | source)
XLA Modules:
  0.0 140.1 jit_solution(8160693846711729315)
XLA Ops:
  0.7 14.3 %front.1 = (s32[3,32]{1,0:T(4,128)}, f32[3,24,8,128]{3,2,1,0:T(8,128)}, bf16[12,256,128]{2,1,0:T(8,128)(2,1)}, bf16[12,256,128]{2,1,0:T(8,128)(2,1)}, f32[2688,1...) custom-call(s32[1,24]{1,0:T(1,128)} %heights.1, ...), custom_call_target="tpu_custom_call" | custom-call | tf_op jit(solution)/shard_map/front/pallas_call | solution.py:1511
  14.9 15.3 %attend.1 = (f32[2688,128]{1,0:T(8,128)}, bf16[2688,128]{1,0:T(8,128)(2,1)}, bf16[2688,128]{1,0:T(8,128)(2,1)}, f32[12,128,256]{2,1,0:T(8,128)}, f32[12,8,256]{2...) custom-call(s32[3,32]{1,0:T(4,128)} %get-tuple-element.75.table, ...), custom_call_target="tpu_custom_call" | custom-call | tf_op jit(solution)/shard_map/attend/pallas_call | solution.py:1543
  30.3 44.6 %hidden.4 = (bf16[2688,128]{1,0:T(8,128)(2,1)}, f32[2688,128]{1,0:T(8,128)}, bf16[12,256,128]{2,1,0:T(8,128)(2,1)}, f32[2,2,544,128]{3,2,1,0:T(8,128)}, f32[136,128]{1,0:T(8,128)}) custom-call(s32[3,32]{1,0:T(4,128)} %get-tuple-element.75.table, f32[2688,128]{1,0:T(8,128)} %get-tuple-element.85.x1_in, bf16[2688,128]{1,0:T(8,128)(2,1)} %get-tuple-element.86.xm, ...), custom_call_target="tpu_custom_call" | custom-call | tf_op jit(solution)/shard_map/hidden/pallas_call | solution.py:1588
  74.9 20.8 %attend_back.1 = (bf16[12,256,128]{2,1,0:T(8,128)(2,1)}, f32[13,80,128]{2,1,0:T(8,128)}, bf16[13,80,128]{2,1,0:T(8,128)(2,1)}, bf16[2688,128]{1,0:T(8,128)(2,1)}) custom-call(s32[3,32]{1,0:T(4,128)} %get-tuple-element.75.table, bf16[24,16,128]{2,1,0:T(8,128)(2,1)} %get-tuple-element.81.key_c, f32[24,56,128]{2,1,0:T(8,128)} %get-tuple-element.82.key_f, ...), custom_call_target="tpu_custom_call" | custom-call | tf_op jit(solution)/shard_map/attend_back/pallas_call | solution.py:1631
  95.7 40.7 %tail.1 = (f32[2688,128]{1,0:T(8,128)}, bf16[2,2,8,176,128]{4,3,2,1,0:T(8,128)(2,1)}, f32[48,128]{1,0:T(8,128)}) custom-call(f32[13,80,128]{2,1,0:T(8,128)} %get-tuple-element.98.own_in, bf16[13,80,128]{2,1,0:T(8,128)(2,1)} %get-tuple-element.99.given, f32[2,2,544,128]{3,2,1,0:T(8,128)} %get-tuple-element.100.split_in, f32[136,128]{1,0:T(8,128)} %get-tuple-element.101.mid_g, ...), custom_call_target="tpu_custom_call" | custom-call | tf_op jit(solution)/shard_map/tail/pallas_call | solution.py:1671
  136.4 3.7 %unpack.1 = (f32[2688,128]{1,0:T(8,128)}, f32[2,128]{1,0:T(2,128)}, f32[4,128]{1,0:T(4,128)}, f32[64,128]{1,0:T(8,128)}, f32[2048,128]{1,0:T(8,128)}, /*index=5*...) custom-call(bf16[2,2,8,176,128]{4,3,2,1,0:T(8,128)(2,1)} %get-tuple-, ...), custom_call_target="tpu_custom_call" | custom-call | tf_op jit(solution)/shard_map/unpack/pallas_call | solution.py:1722

commit v3 on v2

--- a/solution.py
+++ b/solution.py
@@ -989,10 +989,12 @@
         for flips in range(1, 2 ** len(dims)):
             part = mine
             if "x" in dims and flips >> dims.index("x") & 1:
+                if not self.shared:
+                    continue
                 part = self.out.at[self.core, self.side, pl.ds(at, count), pl.ds(0, self.shared)]
             yield self.made(part, number, flipped(self.batch, self.side, dims, flips))
             number += 1
-        if stage == 0:
+        if stage == 0 and self.shared:
             part = self.out.at[self.core, 1 - self.side, :, pl.ds(0, self.shared)]
             yield self.made(part, number, flipped(self.batch, self.side, dims, 1))
 
@@ -1142,7 +1144,7 @@
     query_o, dx1_in, inv_in, gains,
     red_c_in, conv_c_in, gain_c, shifts_c, kv_c, taps_c_ref,
     red_f_in, conv_f_in, gain_f, shifts_f, kv_f, taps_f_ref,
-    tok_grad, joint, little,
+    tok_grad, early, joint, little,
     pack, small, small_in, small_sems, recv, grad_ref, val_ref, dxn, send_sem, recv_sem, send_sems, recv_sems, turned_c, turned_f,
     dx1, inv, hat_ref, own, split_g, slab, xn, dq, red_c, conv_c, red_f, conv_f, xt, load_sems,
     *buffers,
@@ -1174,7 +1176,9 @@
     rest = Group(levels, True, buffers[shared_count:], sems, base)
     base += group_links(levels, True)
     early_rows, late_rows, later_rows = (group.cur.shape[1] for group in (before, conv, rest))
-    gather = Gather(levels, joint, (late_rows + later_rows) // joint.shape[2], sems, base)
+    gather = Gather(levels, joint, joint.shape[3], sems, base)
+    base += group_links(levels, True) + len(stages(levels, True))
+    gather_split = Gather(levels, early, 0, sems, base)
 
     def split_pieces(half, which):
         yield 0, split_g[(half + side) % 2, which]
@@ -1373,7 +1377,9 @@
         back = norm_back(dxn[band] * gains[0:1, :], hat_ref[band].astype(F32), 1.0)
         tok_grad[at, :] = dx1[at, :] + dot(place, back.astype(BF16)) * inv[at, :]
 
-    done, total = 0, len(rest.left) + 1 + len(gather.left)
+    began = len(before.left) + 1
+    done = 0
+    total = max(len(rest.left) + 1 + len(gather.left), began + len(gather_split.left))
     for number in range(1, total + 1):
         while done < bands and done * total < number * bands:
             one_band(done)
@@ -1381,13 +1387,17 @@
         if rest.left:
             rest.advance()
             conv.advance()
-            before.advance()
         elif number + len(gather.left) == total:
             conv.advance(len(conv.left))
-            before.advance(len(before.left))
-            gather.begin([conv.finish(), rest.finish(), before.finish()])
+            gather.begin([conv.finish(), rest.finish()])
         else:
             gather.advance()
+        if before.left:
+            before.advance()
+        elif number == began:
+            gather_split.begin([before.finish()])
+        elif gather_split.left:
+            gather_split.advance()
         if number <= len(order):
             small_phase(number)
 
@@ -1407,21 +1417,34 @@
 
 
 def unpack_kernel(
-    levels,     joint, little, tok_grad,
+    levels,     early, joint, little, tok_grad,
     tok_grad_out, gains, shifts, query, conv_c, gain_c, shifts_c, kv_c, taps_c, conv_f, gain_f, shifts_f, kv_f,
+    taps_f, proj, hidden, fc1, depth, fc2,
+):
+    tok_grad_out[...] = tok_grad[...]
+
+    @pl.when(pl.program_id(0) == 0)
+    def _():
+        unpack_grads(
+            levels, early, joint, little, gains, shifts, query, conv_c, gain_c, shifts_c, kv_c,
+            taps_c, conv_f, gain_f, shifts_f, kv_f, taps_f, proj, hidden, fc1, depth, fc2,
+        )
+
+
+def unpack_grads(
+    levels, early, joint, little,
+    gains, shifts, query, conv_c, gain_c, shifts_c, kv_c, taps_c, conv_f, gain_f, shifts_f, kv_f,
     taps_f, proj, hidden, fc1, depth, fc2,
 ):
     side = lax.axis_index("heads")
     half = query.shape[0]
-    pieces, wide = joint.shape[2], fc2.shape[0]
-    widths = [group_size(levels, part) // pieces for part in (CONV, REST, SPLIT)]
-    first, second = widths[0], widths[0] + widths[1]
-    spans = (slice(0, first), slice(first, second), slice(second, second + widths[2]))
+    first = group_size(levels, CONV) // joint.shape[2]
+    spans = (slice(0, first), slice(first, joint.shape[3]))
 
     def quarter_rows(group, core, h):
-        return joint[core, h, :, spans[group], :].reshape(-1, 128)
-
-    tok_grad_out[...] = tok_grad[...]
+        ref, rows = (early, slice(None)) if group == 2 else (joint, spans[group])
+        return ref[core, h, :, rows, :].reshape(-1, 128)
+
 
     def rows_of(start, count):
         pieces = [
@@ -1664,20 +1687,21 @@
     )(table, key_c, key_f, val_c, val_f, xn, query_t, query_o, out_grad, out_t, lse, output)
 
     peers = sum(2 ** len(dims) - 1 for dims in stages(levels, True))
-    links = group_links(levels, False) + 3 * group_links(levels, True) + len(stages(levels, True)) + 1
+    links = group_links(levels, False) + 4 * group_links(levels, True) + 2 * len(stages(levels, True)) + 1
     early_rows, late_rows, later_rows = (group_size(levels, part) for part in (SPLIT, CONV, REST))
     pieces = 2 ** (levels - 1)
-    joint_rows = (early_rows + late_rows + later_rows) // pieces
-    tokens_grad, joint, little = pl.pallas_call(
+    joint_rows = (late_rows + later_rows) // pieces
+    tokens_grad, early, joint, little = pl.pallas_call(
         functools.partial(tail_kernel, levels),
         out_shape=(
             shape((count, 128)),
+            shape((2, 2, pieces, early_rows // pieces, 128), BF16),
             shape((2, 2, pieces, joint_rows, 128), BF16),
             shape((SMALL, 128)),
         ),
         in_specs=[HBM] * 3 + [VMEM, HBM] + [VMEM] * 2 + [HBM] * 3 + [VMEM] * 2 + [HBM] * 2
         + [VMEM] + ([HBM] * 2 + [VMEM] * 4) * 2,
-        out_specs=[VMEM] * 3,
+        out_specs=[VMEM] * 4,
         scratch_shapes=[
             pltpu.VMEM((4 * QUARTER, 128), F32),
             pltpu.VMEM((len(stages(levels, True)), SMALL, 128), F32),
@@ -1742,11 +1766,12 @@
             shape((9, mine)),
             shape((mine, 128)),
         ),
-        in_specs=[VMEM] * 3,
-        out_specs=[VMEM] * 19,
+        grid=(bands // 2,),
+        in_specs=[VMEM] * 3 + [pl.BlockSpec((2 * BAND, 128), lambda i: (i, 0))],
+        out_specs=[pl.BlockSpec((2 * BAND, 128), lambda i: (i, 0))] + [VMEM] * 18,
         compiler_params=params(),
         name="unpack",
-    )(joint, little, tokens_grad)
+    )(early, joint, little, tokens_grad)
     grads = [output] + list(grads)
     grads[4] = grads[4].T
     for at in (6, 11):

time: 140 us -> 142 us (1.014)
  Pallas kernels: 139 us -> 141 us
    pallas_call x1, Pallas kernels: 3.68 us -> 5.94 us  [per_device(): pl.pallas_call(functools.partial(unpack_kernel, levels), out_shape=(shape...]
where the time goes in v3:
time: 142 us
  Pallas kernels  141 us (99%)
    pallas_call x1, Pallas kernels, per_device(): pl.pallas_call(hidden_kernel, out_shape=(shape((count, 128), BF16), shape...  44.6 us
    pallas_call x1, Pallas kernels, per_device(): pl.pallas_call(functools.partial(tail_kernel, levels), out_shape=(shape((...  40 us
    pallas_call x1, Pallas kernels, per_device(): pl.pallas_call(attend_back_kernel, grid=(bands // 2,), out_shape=(shape((...  20.5 us
    pallas_call x1, Pallas kernels, per_device(): pl.pallas_call(attend_kernel, grid=(bands // each,), out_shape=(shape((co...  15.4 us
    pallas_call x1, Pallas kernels, per_device(): pl.pallas_call(front_kernel, out_shape=(shape((3, 32), jnp.int32), shape(...  14.3 us
    pallas_call x1, Pallas kernels, per_device(): pl.pallas_call(functools.partial(unpack_kernel, levels), out_shape=(shape...  5.94 us

profile of v3, /device:TPU:0, one launch (start us, length us, event | category | flops | bytes accessed | tf_op | source)
XLA Modules:
  0.0 141.7 jit_solution(8465564486532731113)
XLA Ops:
  0.7 14.3 %front.1 = (s32[3,32]{1,0:T(4,128)}, f32[3,24,8,128]{3,2,1,0:T(8,128)}, bf16[12,256,128]{2,1,0:T(8,128)(2,1)}, bf16[12,256,128]{2,1,0:T(8,128)(2,1)}, f32[2688,1...) custom-call(s32[1,24]{1,0:T(1,128)} %heights.1, ...), custom_call_target="tpu_custom_call" | custom-call | tf_op jit(solution)/shard_map/front/pallas_call | solution.py:1534
  14.9 15.4 %attend.1 = (f32[2688,128]{1,0:T(8,128)}, bf16[2688,128]{1,0:T(8,128)(2,1)}, bf16[2688,128]{1,0:T(8,128)(2,1)}, f32[12,128,256]{2,1,0:T(8,128)}, f32[12,8,256]{2...) custom-call(s32[3,32]{1,0:T(4,128)} %get-tuple-element.76.table, ...), custom_call_target="tpu_custom_call" | custom-call | tf_op jit(solution)/shard_map/attend/pallas_call | solution.py:1566
  30.3 44.6 %hidden.4 = (bf16[2688,128]{1,0:T(8,128)(2,1)}, f32[2688,128]{1,0:T(8,128)}, bf16[12,256,128]{2,1,0:T(8,128)(2,1)}, f32[2,2,544,128]{3,2,1,0:T(8,128)}, f32[136,128]{1,0:T(8,128)}) custom-call(s32[3,32]{1,0:T(4,128)} %get-tuple-element.76.table, f32[2688,128]{1,0:T(8,128)} %get-tuple-element.86.x1_in, bf16[2688,128]{1,0:T(8,128)(2,1)} %get-tuple-element.87.xm, ...), custom_call_target="tpu_custom_call" | custom-call | tf_op jit(solution)/shard_map/hidden/pallas_call | solution.py:1611
  74.9 20.5 %attend_back.1 = (bf16[12,256,128]{2,1,0:T(8,128)(2,1)}, f32[13,80,128]{2,1,0:T(8,128)}, bf16[13,80,128]{2,1,0:T(8,128)(2,1)}, bf16[2688,128]{1,0:T(8,128)(2,1)}) custom-call(s32[3,32]{1,0:T(4,128)} %get-tuple-element.76.table, bf16[24,16,128]{2,1,0:T(8,128)(2,1)} %get-tuple-element.82.key_c, f32[24,56,128]{2,1,0:T(8,128)} %get-tuple-element.83.key_f, ...), custom_call_target="tpu_custom_call" | custom-call | tf_op jit(solution)/shard_map/attend_back/pallas_call | solution.py:1654
  95.5 40.0 %tail.1 = (f32[2688,128]{1,0:T(8,128)}, bf16[2,2,8,80,128]{4,3,2,1,0:T(8,128)(2,1)}, bf16[2,2,8,96,128]{4,3,2,1,0:T(8,128)(2,1)}, f32[48,128]{1,0:T(8,128)}) custom-call(f32[13,80,128]{2,1,0:T(8,128)} %get-tuple-element.99.own_in, bf16[13,80,128]{2,1,0:T(8,128)(2,1)} %get-tuple-element.100.given, f32[2,2,544,128]{3,2,1,0:T(8,128)} %get-tuple-element.101.split_in, ...), custom_call_target="tpu_custom_call" | custom-call | tf_op jit(solution)/shard_map/tail/pallas_call | solution.py:1694
  135.5 5.9 %unpack.1 = (f32[2688,128]{1,0:T(8,128)}, f32[2,128]{1,0:T(2,128)}, f32[4,128]{1,0:T(4,128)}, f32[64,128]{1,0:T(8,128)}, f32[2048,128]{1,0:T(8,128)}, /*index=5*...) custom-call(bf16[2,2,8,80,128]{4,3,2,1,0:T(8,128)(2,1)} %get-tuple-e, ...), custom_call_target="tpu_custom_call" | custom-call | tf_op jit(solution)/shard_map/unpack/pallas_call | solution.py:1746

commit v4 on v3

--- a/solution.py
+++ b/solution.py
@@ -1252,7 +1252,6 @@
         total = part if total is None else total + part
     query_g[...] = total
     full = full_query(query_t, query_o, side).astype(BF16)
-    dxn[...] = dot(dq[...].reshape(-1, 128), full).reshape(bands, SLOTS, 128)
     grad_ref[0] = jnp.zeros((CELLS, 128), F32)
     grad_ref[bands + 1] = jnp.zeros((CELLS, 128), F32)
     turned_c[...] = conv_c[...].T
@@ -1300,12 +1299,10 @@
     pair = mid + depthwise_coarse(ext, above, below, taps_c, flip=True)
     pair = jnp.where(cell_valid(pair.shape, 1), pair, 0.0)
     pair = pair.reshape(bands * COARSE, 128).astype(BF16)
-    dc = reduce_back(pair, red_c, conv_c, gain_c, shifts_c, kv_c[...], small_c, kv_c_g)
+    dc_c = reduce_back(pair, red_c, conv_c, gain_c, shifts_c, kv_c[...], small_c, kv_c_g)
     for i in range(16):
         part = slice(i * 128, (i + 1) * 128)
-        conv_c_g[part, :] = dot(xt[i], dc)
-        back = dot(dc, turned_c[:, part]).reshape(bands, 16, 128)
-        dxn[:, 16 * i : 16 * i + 16, :] += back
+        conv_c_g[part, :] = dot(xt[i], dc_c)
 
     conv.advance(1, shared_pieces(0, CONV, late_rows))
     before.advance()
@@ -1340,22 +1337,30 @@
             blocks.append(block.astype(BF16).reshape(bands, 1, 16, 128))
     pair = jnp.concatenate(blocks, axis=1).reshape(bands * FINE, 128)
     conv.advance()
-    dc = reduce_back(pair, red_f, conv_f, gain_f, shifts_f, kv_f_sw, small_f, kv_f_g)
+    dc_f = reduce_back(pair, red_f, conv_f, gain_f, shifts_f, kv_f_sw, small_f, kv_f_g)
+    cells_f = [
+        dc_f.reshape(bands, 4, 16, 128)[:, i].reshape(bands * 16, 128) for i in range(4)
+    ]
     for i in range(4):
         part = slice(i * 128, (i + 1) * 128)
         total = None
         for row in range(2):
             for column in range(2):
-                cells = dc.reshape(bands, 4, 16, 128)[:, 2 * row + column].reshape(bands * 16, 128)
-                product = dot(xt[fine_slot(i, row, column)], cells)
+                product = dot(xt[fine_slot(i, row, column)], cells_f[2 * row + column])
                 total = product if total is None else total + product
         conv_f_g[part, :] = total
-        back = dot(dc, turned_f[:, part]).reshape(bands, 4, 16, 128)
+    rest.advance(1, shared_pieces(4 * CONV, REST, later_rows))
+    conv.advance()
+    before.advance()
+    for part in range(4):
         for row in range(2):
             for column in range(2):
-                slot = 16 * fine_slot(i, row, column)
-                dxn[:, slot : slot + 16, :] += back[:, 2 * row + column]
-
+                slot = fine_slot(part, row, column)
+                left = [slot_grads[:, slot].reshape(bands * 16, 128), dc_c, cells_f[2 * row + column]]
+                right = [full, turned_c[:, slot * 128 : slot * 128 + 128]]
+                right.append(turned_f[:, part * 128 : part * 128 + 128])
+                back = dot(jnp.concatenate(left, axis=1), jnp.concatenate(right, axis=0))
+                dxn[:, 16 * slot : 16 * slot + 16, :] = back.reshape(bands, 16, 128)
     front_g[...] = jnp.zeros(front_g.shape, F32)
     sums = jnp.zeros((8, 128), F32)
     along = jnp.zeros((8, 128), F32)
@@ -1367,9 +1372,6 @@
     front_g[1:2, :] = jnp.sum(sums, axis=0, keepdims=True)
 
     small_phase(0)
-    rest.advance(1, shared_pieces(4 * CONV, REST, later_rows))
-    conv.advance()
-    before.advance()
     place = from_slots()
 
     def one_band(band):
@@ -1423,12 +1425,10 @@
 ):
     tok_grad_out[...] = tok_grad[...]
 
-    @pl.when(pl.program_id(0) == 0)
-    def _():
-        unpack_grads(
-            levels, early, joint, little, gains, shifts, query, conv_c, gain_c, shifts_c, kv_c,
-            taps_c, conv_f, gain_f, shifts_f, kv_f, taps_f, proj, hidden, fc1, depth, fc2,
-        )
+    unpack_grads(
+        levels, early, joint, little, gains, shifts, query, conv_c, gain_c, shifts_c, kv_c, taps_c,
+        conv_f, gain_f, shifts_f, kv_f, taps_f, proj, hidden, fc1, depth, fc2,
+    )
 
 
 def unpack_grads(
@@ -1766,9 +1766,8 @@
             shape((9, mine)),
             shape((mine, 128)),
         ),
-        grid=(bands // 2,),
-        in_specs=[VMEM] * 3 + [pl.BlockSpec((2 * BAND, 128), lambda i: (i, 0))],
-        out_specs=[pl.BlockSpec((2 * BAND, 128), lambda i: (i, 0))] + [VMEM] * 18,
+        in_specs=[VMEM] * 4,
+        out_specs=[VMEM] * 19,
         compiler_params=params(),
         name="unpack",
     )(early, joint, little, tokens_grad)

time: 142 us -> 140 us (0.986)
  Pallas kernels: 141 us -> 139 us
    pallas_call x1, Pallas kernels: 5.94 us -> 3.69 us  [per_device(): pl.pallas_call(functools.partial(unpack_kernel, levels), out_shape=(shape...]
where the time goes in v4:
time: 140 us
  Pallas kernels  139 us (99%)
    pallas_call x1, Pallas kernels, per_device(): pl.pallas_call(hidden_kernel, out_shape=(shape((count, 128), BF16), shape...  44.6 us
    pallas_call x1, Pallas kernels, per_device(): pl.pallas_call(functools.partial(tail_kernel, levels), out_shape=(shape((...  40.8 us
    pallas_call x1, Pallas kernels, per_device(): pl.pallas_call(attend_back_kernel, grid=(bands // 2,), out_shape=(shape((...  20.8 us
    pallas_call x1, Pallas kernels, per_device(): pl.pallas_call(attend_kernel, grid=(bands // each,), out_shape=(shape((co...  15.2 us
    pallas_call x1, Pallas kernels, per_device(): pl.pallas_call(front_kernel, out_shape=(shape((3, 32), jnp.int32), shape(...  14.3 us
    pallas_call x1, Pallas kernels, per_device(): pl.pallas_call(functools.partial(unpack_kernel, levels), out_shape=(shape...  3.69 us

profile of v4, /device:TPU:0, one launch (start us, length us, event | category | flops | bytes accessed | tf_op | source)
XLA Modules:
  0.0 140.2 jit_solution(9543253543038320508)
XLA Ops:
  0.7 14.3 %front.1 = (s32[3,32]{1,0:T(4,128)}, f32[3,24,8,128]{3,2,1,0:T(8,128)}, bf16[12,256,128]{2,1,0:T(8,128)(2,1)}, bf16[12,256,128]{2,1,0:T(8,128)(2,1)}, f32[2688,1...) custom-call(s32[1,24]{1,0:T(1,128)} %heights.1, ...), custom_call_target="tpu_custom_call" | custom-call | tf_op jit(solution)/shard_map/front/pallas_call | solution.py:1534
  14.9 15.2 %attend.1 = (f32[2688,128]{1,0:T(8,128)}, bf16[2688,128]{1,0:T(8,128)(2,1)}, bf16[2688,128]{1,0:T(8,128)(2,1)}, f32[12,128,256]{2,1,0:T(8,128)}, f32[12,8,256]{2...) custom-call(s32[3,32]{1,0:T(4,128)} %get-tuple-element.76.table, ...), custom_call_target="tpu_custom_call" | custom-call | tf_op jit(solution)/shard_map/attend/pallas_call | solution.py:1566
  30.1 44.6 %hidden.4 = (bf16[2688,128]{1,0:T(8,128)(2,1)}, f32[2688,128]{1,0:T(8,128)}, bf16[12,256,128]{2,1,0:T(8,128)(2,1)}, f32[2,2,544,128]{3,2,1,0:T(8,128)}, f32[136,128]{1,0:T(8,128)}) custom-call(s32[3,32]{1,0:T(4,128)} %get-tuple-element.76.table, f32[2688,128]{1,0:T(8,128)} %get-tuple-element.86.x1_in, bf16[2688,128]{1,0:T(8,128)(2,1)} %get-tuple-element.87.xm, ...), custom_call_target="tpu_custom_call" | custom-call | tf_op jit(solution)/shard_map/hidden/pallas_call | solution.py:1611
  74.8 20.8 %attend_back.1 = (bf16[12,256,128]{2,1,0:T(8,128)(2,1)}, f32[13,80,128]{2,1,0:T(8,128)}, bf16[13,80,128]{2,1,0:T(8,128)(2,1)}, bf16[2688,128]{1,0:T(8,128)(2,1)}) custom-call(s32[3,32]{1,0:T(4,128)} %get-tuple-element.76.table, bf16[24,16,128]{2,1,0:T(8,128)(2,1)} %get-tuple-element.82.key_c, f32[24,56,128]{2,1,0:T(8,128)} %get-tuple-element.83.key_f, ...), custom_call_target="tpu_custom_call" | custom-call | tf_op jit(solution)/shard_map/attend_back/pallas_call | solution.py:1654
  95.6 40.8 %tail.1 = (f32[2688,128]{1,0:T(8,128)}, bf16[2,2,8,80,128]{4,3,2,1,0:T(8,128)(2,1)}, bf16[2,2,8,96,128]{4,3,2,1,0:T(8,128)(2,1)}, f32[48,128]{1,0:T(8,128)}) custom-call(f32[13,80,128]{2,1,0:T(8,128)} %get-tuple-element.99.own_in, bf16[13,80,128]{2,1,0:T(8,128)(2,1)} %get-tuple-element.100.given, f32[2,2,544,128]{3,2,1,0:T(8,128)} %get-tuple-element.101.split_in, ...), custom_call_target="tpu_custom_call" | custom-call | tf_op jit(solution)/shard_map/tail/pallas_call | solution.py:1694
  136.4 3.7 %unpack.1 = (f32[2688,128]{1,0:T(8,128)}, f32[2,128]{1,0:T(2,128)}, f32[4,128]{1,0:T(4,128)}, f32[64,128]{1,0:T(8,128)}, f32[2048,128]{1,0:T(8,128)}, /*index=5*...) custom-call(bf16[2,2,8,80,128]{4,3,2,1,0:T(8,128)(2,1)} %get-tuple-e, ...), custom_call_target="tpu_custom_call" | custom-call | tf_op jit(solution)/shard_map/unpack/pallas_call | solution.py:1746

commit v5 on v3

--- a/solution.py
+++ b/solution.py
@@ -1423,12 +1423,10 @@
 ):
     tok_grad_out[...] = tok_grad[...]
 
-    @pl.when(pl.program_id(0) == 0)
-    def _():
-        unpack_grads(
-            levels, early, joint, little, gains, shifts, query, conv_c, gain_c, shifts_c, kv_c,
-            taps_c, conv_f, gain_f, shifts_f, kv_f, taps_f, proj, hidden, fc1, depth, fc2,
-        )
+    unpack_grads(
+        levels, early, joint, little, gains, shifts, query, conv_c, gain_c, shifts_c, kv_c, taps_c,
+        conv_f, gain_f, shifts_f, kv_f, taps_f, proj, hidden, fc1, depth, fc2,
+    )
 
 
 def unpack_grads(
@@ -1559,7 +1557,8 @@
     each = 4 if bands % 4 == 0 else 2
     some_bands = pl.BlockSpec((each * BAND, 128), lambda i: (i, 0))
     some_slots = pl.BlockSpec((each, SLOTS, 128), lambda i: (i, 0, 0))
-    two_slots = pl.BlockSpec((2, SLOTS, 128), lambda i: (i, 0, 0))
+    back = 3 if bands % 3 == 0 else 2
+    back_slots = pl.BlockSpec((back, SLOTS, 128), lambda i: (i, 0, 0))
     (
         x1, xm, heads_out, out_t, lse, key_c, key_f, val_c, val_f, fc1_o, fc2_o, depth_o, hidden_o,
         cot_o,
@@ -1653,7 +1652,7 @@
 
     dq, grad_own, grad_send, output = pl.pallas_call(
         attend_back_kernel,
-        grid=(bands // 2,),
+        grid=(bands // back,),
         out_shape=(
             shape((bands, SLOTS, 128), BF16),
             shape((bands + 1, CELLS, 128)),
@@ -1663,24 +1662,24 @@
         in_specs=[SMEM]
         + [VMEM] * 4
         + [
-            two_slots,
+            back_slots,
             VMEM,
             VMEM,
-            two_slots,
-            pl.BlockSpec((2, 128, SLOTS), lambda i: (i, 0, 0)),
-            pl.BlockSpec((2, 8, SLOTS), lambda i: (i, 0, 0)),
-            pl.BlockSpec((2 * BAND, 128), lambda i: (i, 0)),
+            back_slots,
+            pl.BlockSpec((back, 128, SLOTS), lambda i: (i, 0, 0)),
+            pl.BlockSpec((back, 8, SLOTS), lambda i: (i, 0, 0)),
+            pl.BlockSpec((back * BAND, 128), lambda i: (i, 0)),
         ],
-        out_specs=[two_slots, VMEM, VMEM, pl.BlockSpec((2 * BAND, 128), lambda i: (i, 0))],
+        out_specs=[back_slots, VMEM, VMEM, pl.BlockSpec((back * BAND, 128), lambda i: (i, 0))],
         scratch_shapes=[
             pltpu.VMEM((total, COARSE, 128), F32),
             pltpu.VMEM((total, FINE, 128), F32),
             pltpu.VMEM((128, 128), BF16),
-            pltpu.VMEM((2, 64, MAX_BANDS * COARSE), BF16),
-            pltpu.VMEM((2, 2, 64, HALVES[0][1] * PACKED), BF16),
-            pltpu.VMEM((2, MAX_BANDS * PACKED, 128), BF16),
-            pltpu.VMEM((2, MAX_BANDS * PACKED, 128), BF16),
-            pltpu.SMEM((2,), jnp.int32),
+            pltpu.VMEM((back, 64, MAX_BANDS * COARSE), BF16),
+            pltpu.VMEM((back, 2, 64, HALVES[0][1] * PACKED), BF16),
+            pltpu.VMEM((back, MAX_BANDS * PACKED, 128), BF16),
+            pltpu.VMEM((back, MAX_BANDS * PACKED, 128), BF16),
+            pltpu.SMEM((back,), jnp.int32),
         ],
         compiler_params=params(),
         name="attend_back",
@@ -1766,9 +1765,8 @@
             shape((9, mine)),
             shape((mine, 128)),
         ),
-        grid=(bands // 2,),
-        in_specs=[VMEM] * 3 + [pl.BlockSpec((2 * BAND, 128), lambda i: (i, 0))],
-        out_specs=[pl.BlockSpec((2 * BAND, 128), lambda i: (i, 0))] + [VMEM] * 18,
+        in_specs=[VMEM] * 4,
+        out_specs=[VMEM] * 19,
         compiler_params=params(),
         name="unpack",
     )(early, joint, little, tokens_grad)

time: 142 us -> 139 us (0.979)
  Pallas kernels: 141 us -> 138 us
    pallas_call x1, Pallas kernels: 5.94 us -> 3.69 us  [per_device(): pl.pallas_call(functools.partial(unpack_kernel, levels), out_shape=(shape...]
where the time goes in v5:
time: 139 us
  Pallas kernels  138 us (99%)
    pallas_call x1, Pallas kernels, per_device(): pl.pallas_call(hidden_kernel, out_shape=(shape((count, 128), BF16), shape...  44.6 us
    pallas_call x1, Pallas kernels, per_device(): pl.pallas_call(functools.partial(tail_kernel, levels), out_shape=(shape((...  40 us
    pallas_call x1, Pallas kernels, per_device(): pl.pallas_call(attend_back_kernel, grid=(bands // back,), out_shape=(shap...  20.5 us
    pallas_call x1, Pallas kernels, per_device(): pl.pallas_call(attend_kernel, grid=(bands // each,), out_shape=(shape((co...  15.3 us
    pallas_call x1, Pallas kernels, per_device(): pl.pallas_call(front_kernel, out_shape=(shape((3, 32), jnp.int32), shape(...  14.3 us
    pallas_call x1, Pallas kernels, per_device(): pl.pallas_call(functools.partial(unpack_kernel, levels), out_shape=(shape...  3.69 us

profile of v5, /device:TPU:0, one launch (start us, length us, event | category | flops | bytes accessed | tf_op | source)
XLA Modules:
  0.0 139.2 jit_solution(9655883426727303395)
XLA Ops:
  0.7 14.3 %front.1 = (s32[3,32]{1,0:T(4,128)}, f32[3,24,8,128]{3,2,1,0:T(8,128)}, bf16[12,256,128]{2,1,0:T(8,128)(2,1)}, bf16[12,256,128]{2,1,0:T(8,128)(2,1)}, f32[2688,1...) custom-call(s32[1,24]{1,0:T(1,128)} %heights.1, ...), custom_call_target="tpu_custom_call" | custom-call | tf_op jit(solution)/shard_map/front/pallas_call | solution.py:1532
  14.9 15.3 %attend.1 = (f32[2688,128]{1,0:T(8,128)}, bf16[2688,128]{1,0:T(8,128)(2,1)}, bf16[2688,128]{1,0:T(8,128)(2,1)}, f32[12,128,256]{2,1,0:T(8,128)}, f32[12,8,256]{2...) custom-call(s32[3,32]{1,0:T(4,128)} %get-tuple-element.76.table, ...), custom_call_target="tpu_custom_call" | custom-call | tf_op jit(solution)/shard_map/attend/pallas_call | solution.py:1565
  30.2 44.6 %hidden.4 = (bf16[2688,128]{1,0:T(8,128)(2,1)}, f32[2688,128]{1,0:T(8,128)}, bf16[12,256,128]{2,1,0:T(8,128)(2,1)}, f32[2,2,544,128]{3,2,1,0:T(8,128)}, f32[136,128]{1,0:T(8,128)}) custom-call(s32[3,32]{1,0:T(4,128)} %get-tuple-element.76.table, f32[2688,128]{1,0:T(8,128)} %get-tuple-element.86.x1_in, bf16[2688,128]{1,0:T(8,128)(2,1)} %get-tuple-element.87.xm, ...), custom_call_target="tpu_custom_call" | custom-call | tf_op jit(solution)/shard_map/hidden/pallas_call | solution.py:1610
  74.9 20.5 %attend_back.1 = (bf16[12,256,128]{2,1,0:T(8,128)(2,1)}, f32[13,80,128]{2,1,0:T(8,128)}, bf16[13,80,128]{2,1,0:T(8,128)(2,1)}, bf16[2688,128]{1,0:T(8,128)(2,1)}) custom-call(s32[3,32]{1,0:T(4,128)} %get-tuple-element.76.table, bf16[24,16,128]{2,1,0:T(8,128)(2,1)} %get-tuple-element.82.key_c, f32[24,56,128]{2,1,0:T(8,128)} %get-tuple-element.83.key_f, ...), custom_call_target="tpu_custom_call" | custom-call | tf_op jit(solution)/shard_map/attend_back/pallas_call | solution.py:1653
  95.4 40.0 %tail.1 = (f32[2688,128]{1,0:T(8,128)}, bf16[2,2,8,80,128]{4,3,2,1,0:T(8,128)(2,1)}, bf16[2,2,8,96,128]{4,3,2,1,0:T(8,128)(2,1)}, f32[48,128]{1,0:T(8,128)}) custom-call(f32[13,80,128]{2,1,0:T(8,128)} %get-tuple-element.99.own_in, bf16[13,80,128]{2,1,0:T(8,128)(2,1)} %get-tuple-element.100.given, f32[2,2,544,128]{3,2,1,0:T(8,128)} %get-tuple-element.101.split_in, ...), custom_call_target="tpu_custom_call" | custom-call | tf_op jit(solution)/shard_map/tail/pallas_call | solution.py:1693
  135.4 3.7 %unpack.1 = (f32[2688,128]{1,0:T(8,128)}, f32[2,128]{1,0:T(2,128)}, f32[4,128]{1,0:T(4,128)}, f32[64,128]{1,0:T(8,128)}, f32[2048,128]{1,0:T(8,128)}, /*index=5*...) custom-call(bf16[2,2,8,80,128]{4,3,2,1,0:T(8,128)(2,1)} %get-tuple-e, ...), custom_call_target="tpu_custom_call" | custom-call | tf_op jit(solution)/shard_map/unpack/pallas_call | solution.py:1745
